TPU v7x, 128 devices: a whole 4x4x4 slice. The times are simulated.
128 devices in a mesh: pipe: 2 (over y_lo), shard: 32 (over z, x, core), tensor: 2 (over y_hi).
Axes of the slice: x: 4, y: 4 (y_hi: 2, y_lo: 2; y = y_hi * 2 + y_lo), z: 4, core: 2. Of those that a mesh axis runs over, the one named last changes fastest.
Arguments:
- clip_frames: bfloat16 [4, 6144, 768], P(None, 'shard'), may hold values from -6 to 6
- out_cotangent: bfloat16 [4, 6144, 768], P(None, 'shard'), may hold values from -6 to 6
- clip_lengths: int32 [4, 32], P(None, 'shard'), may hold values from 48 to 192, as said below
- query_weight: bfloat16 [2, 768, 768], P('pipe', 'shard', 'tensor'), may hold values from -0.21875 to 0.21875
- key_weight: bfloat16 [2, 768, 768], P('pipe', 'shard', 'tensor'), may hold values from -0.21875 to 0.21875
- value_weight: bfloat16 [2, 768, 768], P('pipe', 'shard', 'tensor'), may hold values from -0.21875 to 0.21875
- output_weight: bfloat16 [2, 768, 768], P('pipe', 'shard', 'tensor'), may hold values from -0.875 to 0.875
- up_weight: bfloat16 [2, 768, 3072], P('pipe', 'shard', 'tensor'), may hold values from -0.21875 to 0.21875
- down_weight: bfloat16 [2, 768, 3072], P('pipe', 'shard', 'tensor'), may hold values from -0.15625 to 0.15625
- query_bias: bfloat16 [2, 64, 12], P('pipe', 'shard', 'tensor'), may hold values from -3 to 3
- value_bias: bfloat16 [2, 64, 12], P('pipe', 'shard', 'tensor'), may hold values from -3 to 3
- output_bias: bfloat16 [2, 768], P('pipe', 'shard'), may hold values from -3 to 3
- up_bias: bfloat16 [2, 64, 48], P('pipe', 'shard', 'tensor'), may hold values from -3 to 3
- down_bias: bfloat16 [2, 768], P('pipe', 'shard'), may hold values from -3 to 3
- first_gain: bfloat16 [2, 768], P('pipe', 'shard'), may hold values from 0.5 to 1.5
- first_shift: bfloat16 [2, 768], P('pipe', 'shard'), may hold values from -2 to 2
- second_gain: bfloat16 [2, 768], P('pipe', 'shard'), may hold values from 0.5 to 1.5
- second_shift: bfloat16 [2, 768], P('pipe', 'shard'), may hold values from -2 to 2
Outputs:
- section_output: bfloat16 [2, 4, 6144, 768], P('pipe', None, 'shard')
- input_grad: bfloat16 [2, 4, 6144, 768], P('pipe', None, 'shard')
- query_weight_grad: float32 [2, 768, 768], P('pipe', 'shard', 'tensor')
- key_weight_grad: float32 [2, 768, 768], P('pipe', 'shard', 'tensor')
- value_weight_grad: float32 [2, 768, 768], P('pipe', 'shard', 'tensor')
- output_weight_grad: float32 [2, 768, 768], P('pipe', 'shard', 'tensor')
- up_weight_grad: float32 [2, 768, 3072], P('pipe', 'shard', 'tensor')
- down_weight_grad: float32 [2, 768, 3072], P('pipe', 'shard', 'tensor')
- query_bias_grad: float32 [2, 64, 12], P('pipe', 'shard', 'tensor')
- value_bias_grad: float32 [2, 64, 12], P('pipe', 'shard', 'tensor')
- output_bias_grad: float32 [2, 768], P('pipe', 'shard')
- up_bias_grad: float32 [2, 64, 48], P('pipe', 'shard', 'tensor')
- down_bias_grad: float32 [2, 768], P('pipe', 'shard')
- first_gain_grad: float32 [2, 768], P('pipe', 'shard')
- first_shift_grad: float32 [2, 768], P('pipe', 'shard')
- second_gain_grad: float32 [2, 768], P('pipe', 'shard')
- second_shift_grad: float32 [2, 768], P('pipe', 'shard')
Inputs may be any that keep to these rules, and one draw needn't show every extreme that they name: `clip_lengths`: frames of a clip at or past its length are padding and are not attended to as keys; some clip of the batch has all 192 frames.
All inputs are finite; a program needn't handle non-finite values.
Results may differ from a plain program's by a relative error of at most 0.033.
Values may be sent and summed in bfloat16 or wider, within the bound.
No kernel may reach another device: no remote copies, remote signals or barrier semaphores. Data moves between devices by JAX's collectives and lax.ppermute only.
A program may use at most 192 MiB of HBM per device.

v0:
```python
import jax
import jax.numpy as jnp
from jax import lax
from jax.sharding import PartitionSpec as P

HEAD = 64
GROUP = 64


half_root = 0.7071067811865476
gauss_factor = 0.3989422804014327


def shortened(array):
    return jax.tree.map(lambda a: a.astype(jnp.bfloat16) if a.dtype == jnp.float32 else a, array)


def passed_along(value, axis, steps):
    count = lax.axis_size(axis)
    first, last = (max(0, -steps), min(count, count - steps))
    return lax.ppermute(value, axis, [(source, source + steps) for source in range(first, last)])


def contract_rows(left_side, right_side):
    return lax.dot_general(
        left_side, right_side, (((0,), (0,)), ((), ())), preferred_element_type=jnp.float32
    )


def contract_cols(left_side, right_side):
    return lax.dot_general(
        left_side, right_side, (((1,), (1,)), ((), ())), preferred_element_type=jnp.float32
    )


def norm_forward(values, norm_gain, norm_shift):
    center = values - jnp.mean(values, -1, keepdims=True)
    rescale = lax.rsqrt(jnp.mean(center * center, -1, keepdims=True) + 1e-05)
    normed = center * rescale
    return (normed * norm_gain + norm_shift, normed, rescale)


def norm_backward(grad_rows, normed, rescale, norm_gain):
    scaled = grad_rows * norm_gain
    inner = (
        scaled
        - jnp.mean(scaled, -1, keepdims=True)
        - normed * jnp.mean(scaled * normed, -1, keepdims=True)
    )
    return (rescale * inner, jnp.sum(grad_rows * normed, 0), jnp.sum(grad_rows, 0))


def gelu_slope(pre_active):
    return (
        0.5 * (1.0 + lax.erf(pre_active * half_root))
        + pre_active * jnp.exp(-0.5 * pre_active * pre_active) * gauss_factor
    )


def split_heads(row_block):
    return row_block.reshape(row_block.shape[0], -1, HEAD)


def scores_of(query_b, key_b, length):
    row_count = query_b.shape[0]
    scores = jnp.einsum(
        "qhd,khd->hqk", split_heads(query_b), split_heads(key_b), preferred_element_type=jnp.float32
    ) * HEAD ** (-0.5)
    live_keys = (jnp.arange(row_count) < length)[None, None, :]
    return jnp.where(live_keys, scores, -1e30)


def attend(query_b, key_b, value_b, length):
    scores = scores_of(query_b, key_b, length)
    top_score = jnp.max(scores, -1, keepdims=True)
    powers = jnp.exp(scores - top_score)
    row_total = jnp.sum(powers, -1, keepdims=True)
    weights_b = (powers / row_total).astype(jnp.bfloat16)
    mixed_rows = jnp.einsum(
        "hqk,khd->qhd", weights_b, split_heads(value_b), preferred_element_type=jnp.float32
    )
    return (mixed_rows.reshape(query_b.shape[0], -1), top_score + jnp.log(row_total))


def attend_back(query_b, key_b, value_b, log_total, grad_b, length):
    row_count = query_b.shape[0]
    scores = scores_of(query_b, key_b, length)
    weights_soft = jnp.exp(scores - log_total)
    weights_b = weights_soft.astype(jnp.bfloat16)
    grad_heads = split_heads(grad_b)
    grad_weights = jnp.einsum(
        "qhd,khd->hqk", grad_heads, split_heads(value_b), preferred_element_type=jnp.float32
    )
    grad_scores = weights_soft * (
        grad_weights - jnp.sum(grad_weights * weights_soft, -1, keepdims=True)
    )
    grad_scores_b = grad_scores.astype(jnp.bfloat16)
    factor = HEAD ** (-0.5)
    grad_query = (
        jnp.einsum(
            "hqk,khd->qhd", grad_scores_b, split_heads(key_b), preferred_element_type=jnp.float32
        )
        * factor
    )
    grad_key = (
        jnp.einsum(
            "hqk,qhd->khd", grad_scores_b, split_heads(query_b), preferred_element_type=jnp.float32
        )
        * factor
    )
    grad_value = jnp.einsum(
        "hqk,qhd->khd", weights_b, grad_heads, preferred_element_type=jnp.float32
    )
    return (
        grad_query.reshape(row_count, -1).astype(jnp.bfloat16),
        grad_key.reshape(row_count, -1).astype(jnp.bfloat16),
        grad_value.reshape(row_count, -1).astype(jnp.bfloat16),
    )


def prepare(gathered):
    (
        w_query,
        w_key,
        w_value,
        w_out,
        w_up,
        w_down,
        b_query,
        b_value,
        b_out,
        b_up,
        b_down,
        gain_one,
        shift_one,
        gain_two,
        shift_two,
    ) = gathered
    return (
        w_query,
        w_key,
        w_value,
        w_out,
        w_up,
        w_down,
        b_query.astype(jnp.float32).T.reshape(-1),
        b_value.astype(jnp.float32).T.reshape(-1),
        b_out.astype(jnp.float32),
        b_up.astype(jnp.float32).T.reshape(-1),
        b_down.astype(jnp.float32),
        gain_one.astype(jnp.float32),
        shift_one.astype(jnp.float32),
        gain_two.astype(jnp.float32),
        shift_two.astype(jnp.float32),
    )


def layer_forward(section_in, length, weights):
    (
        w_query,
        w_key,
        w_value,
        w_out,
        w_up,
        w_down,
        b_query,
        b_value,
        b_out,
        b_up,
        b_down,
        gain_one,
        shift_one,
        gain_two,
        shift_two,
    ) = weights
    normed, unit_one, scale_one = norm_forward(section_in, gain_one, shift_one)
    normed_b = normed.astype(jnp.bfloat16)
    query_b = (jnp.dot(normed_b, w_query, preferred_element_type=jnp.float32) + b_query).astype(
        jnp.bfloat16
    )
    key_b = jnp.dot(normed_b, w_key, preferred_element_type=jnp.float32).astype(jnp.bfloat16)
    value_b = (jnp.dot(normed_b, w_value, preferred_element_type=jnp.float32) + b_value).astype(
        jnp.bfloat16
    )
    mixed_rows, log_total = attend(query_b, key_b, value_b, length)
    mixed_b = mixed_rows.astype(jnp.bfloat16)
    head_total = lax.psum(contract_cols(mixed_b, w_out), "tensor")
    middle = section_in + head_total + b_out
    normed_two, unit_two, scale_two = norm_forward(middle, gain_two, shift_two)
    normed_two_b = normed_two.astype(jnp.bfloat16)
    pre_active = jnp.dot(normed_two_b, w_up, preferred_element_type=jnp.float32) + b_up
    active_b = jax.nn.gelu(pre_active, approximate=False).astype(jnp.bfloat16)
    unit_total = lax.psum(contract_cols(active_b, w_down), "tensor")
    result = middle + unit_total + b_down
    kept_state = (
        normed_b,
        unit_one,
        scale_one,
        query_b,
        key_b,
        value_b,
        log_total,
        mixed_b,
        unit_two,
        scale_two,
        normed_two_b,
        pre_active,
        active_b,
    )
    return (result, kept_state)


def layer_backward(grad_rows, length, kept_state, weights):
    (
        w_query,
        w_key,
        w_value,
        w_out,
        w_up,
        w_down,
        b_query,
        b_value,
        b_out,
        b_up,
        b_down,
        gain_one,
        shift_one,
        gain_two,
        shift_two,
    ) = weights
    (
        normed_b,
        unit_one,
        scale_one,
        query_b,
        key_b,
        value_b,
        log_total,
        mixed_b,
        unit_two,
        scale_two,
        normed_two_b,
        pre_active,
        active_b,
    ) = kept_state
    grad_b = grad_rows.astype(jnp.bfloat16)
    down_bias_term = jnp.sum(grad_rows, 0)
    down_term = contract_rows(grad_b, active_b)
    grad_active = jnp.dot(grad_b, w_down, preferred_element_type=jnp.float32)
    grad_upper_b = (grad_active * gelu_slope(pre_active)).astype(jnp.bfloat16)
    up_bias_term = jnp.sum(grad_upper_b, 0, dtype=jnp.float32)
    up_term = contract_rows(normed_two_b, grad_upper_b)
    grad_normed_two = lax.psum(
        contract_cols(grad_upper_b, w_up).astype(jnp.bfloat16), "tensor"
    ).astype(jnp.float32)
    grad_norm_two, gain_two_term, shift_two_term = norm_backward(
        grad_normed_two, unit_two, scale_two, gain_two
    )
    grad_middle = grad_rows + grad_norm_two
    out_bias_term = jnp.sum(grad_middle, 0)
    grad_middle_b = grad_middle.astype(jnp.bfloat16)
    out_term = contract_rows(grad_middle_b, mixed_b)
    grad_mixed_b = jnp.dot(grad_middle_b, w_out, preferred_element_type=jnp.float32).astype(
        jnp.bfloat16
    )
    grad_query_b, grad_key_b, grad_value_b = attend_back(
        query_b, key_b, value_b, log_total, grad_mixed_b, length
    )
    query_bias_term = jnp.sum(grad_query_b, 0, dtype=jnp.float32)
    value_bias_term = jnp.sum(grad_value_b, 0, dtype=jnp.float32)
    query_term = contract_rows(normed_b, grad_query_b)
    key_term = contract_rows(normed_b, grad_key_b)
    value_term = contract_rows(normed_b, grad_value_b)
    partial_normed = (
        contract_cols(grad_query_b, w_query)
        + contract_cols(grad_key_b, w_key)
        + contract_cols(grad_value_b, w_value)
    )
    grad_normed = lax.psum(partial_normed.astype(jnp.bfloat16), "tensor").astype(jnp.float32)
    grad_norm_one, gain_one_term, shift_one_term = norm_backward(
        grad_normed, unit_one, scale_one, gain_one
    )
    grad_input = grad_middle + grad_norm_one
    grad_terms = (
        query_term,
        key_term,
        value_term,
        out_term,
        up_term,
        down_term,
        query_bias_term,
        value_bias_term,
        out_bias_term,
        up_bias_term,
        down_bias_term,
        gain_one_term,
        shift_one_term,
        gain_two_term,
        shift_two_term,
    )
    return (grad_input, grad_terms)


def arrange_one(slot, term):
    if slot == 6 or slot == 7:
        return term.reshape(-1, HEAD).T
    if slot == 9:
        return term.reshape(-1, GROUP).T
    return term


def arrange(grad_terms):
    return tuple((arrange_one(slot, term) for slot, term in enumerate(grad_terms)))


def add_trees(left_side, right_side):
    return tuple(
        (first_item + second_item for first_item, second_item in zip(left_side, right_side))
    )


def local(
    clip_frames,
    out_cotangent,
    clip_lengths,
    query_weight,
    key_weight,
    value_weight,
    output_weight,
    up_weight,
    down_weight,
    query_bias,
    value_bias,
    output_bias,
    up_bias,
    down_bias,
    first_gain,
    first_shift,
    second_gain,
    second_shift,
):
    local_params = tuple(
        (
            array_item[0]
            for array_item in (
                query_weight,
                key_weight,
                value_weight,
                output_weight,
                up_weight,
                down_weight,
                query_bias,
                value_bias,
                output_bias,
                up_bias,
                down_bias,
                first_gain,
                first_shift,
                second_gain,
                second_shift,
            )
        )
    )
    section_index = lax.axis_index("pipe")
    micro_count = clip_frames.shape[0]
    weights = prepare(
        jax.tree.map(
            lambda part, own: part.astype(own.dtype),
            lax.all_gather(shortened(local_params), "shard", axis=0, tiled=True),
            local_params,
        )
    )
    arrived = jnp.zeros(clip_frames.shape[1:], jnp.bfloat16)
    results = []
    kept_list = []
    for turn_index in range(micro_count + 1):
        own_rows = clip_frames[min(turn_index, micro_count - 1)].astype(jnp.float32)
        section_in = jnp.where(section_index == 0, own_rows, arrived.astype(jnp.float32))
        length = clip_lengths[jnp.clip(turn_index - section_index, 0, micro_count - 1), 0]
        result, kept_state = layer_forward(section_in, length, weights)
        result_b = result.astype(jnp.bfloat16)
        if turn_index < micro_count:
            arrived = passed_along(result_b, "pipe", 1)
        results.append(result_b)
        kept_list.append(kept_state)
    section_output = jnp.stack(
        [
            jnp.where(section_index == 0, results[micro_index], results[micro_index + 1])
            for micro_index in range(micro_count)
        ]
    )[None]
    stacked_state = jax.tree.map(lambda *leaves: jnp.stack(leaves), *kept_list)
    returned = jnp.zeros(clip_frames.shape[1:], jnp.bfloat16)
    grad_list = []
    totals = None
    final_shares = None
    for turn_index in range(micro_count + 1):
        if turn_index < micro_count:
            outer_grad = out_cotangent[turn_index].astype(jnp.float32)
        else:
            outer_grad = jnp.zeros(clip_frames.shape[1:], jnp.float32)
        grad_in = jnp.where(section_index == 1, outer_grad, returned.astype(jnp.float32))
        pick_index = jnp.clip(turn_index - 1 + 2 * section_index, 0, micro_count)
        kept_state = jax.tree.map(
            lambda member: lax.dynamic_index_in_dim(member, pick_index, 0, keepdims=False),
            stacked_state,
        )
        length = clip_lengths[jnp.clip(turn_index - 1 + section_index, 0, micro_count - 1), 0]
        grad_input, grad_terms = layer_backward(grad_in, length, kept_state, weights)
        totals = grad_terms if totals is None else add_trees(totals, grad_terms)
        grad_input_b = grad_input.astype(jnp.bfloat16)
        if turn_index < micro_count:
            returned = passed_along(grad_input_b, "pipe", -1)
        grad_list.append(grad_input_b)
    input_grad = jnp.stack(
        [
            jnp.where(section_index == 1, grad_list[micro_index], grad_list[micro_index + 1])
            for micro_index in range(micro_count)
        ]
    )[None]
    final_shares = jax.tree.map(
        lambda part: part.astype(jnp.float32),
        lax.psum_scatter(shortened(arrange(totals)), "shard", scatter_dimension=0, tiled=True),
    )
    return (section_output, input_grad) + tuple((share_item[None] for share_item in final_shares))


def solution(mesh):
    return jax.shard_map(
        local,
        mesh=mesh,
        in_specs=(
            P(None, "shard", None),
            P(None, "shard", None),
            P(None, "shard"),
            P("pipe", "shard", "tensor"),
            P("pipe", "shard", "tensor"),
            P("pipe", "shard", "tensor"),
            P("pipe", "shard", "tensor"),
            P("pipe", "shard", "tensor"),
            P("pipe", "shard", "tensor"),
            P("pipe", "shard", "tensor"),
            P("pipe", "shard", "tensor"),
            P("pipe", "shard"),
            P("pipe", "shard", "tensor"),
            P("pipe", "shard"),
            P("pipe", "shard"),
            P("pipe", "shard"),
            P("pipe", "shard"),
            P("pipe", "shard"),
        ),
        out_specs=(
            P("pipe", None, "shard", None),
            P("pipe", None, "shard", None),
            P("pipe", "shard", "tensor"),
            P("pipe", "shard", "tensor"),
            P("pipe", "shard", "tensor"),
            P("pipe", "shard", "tensor"),
            P("pipe", "shard", "tensor"),
            P("pipe", "shard", "tensor"),
            P("pipe", "shard", "tensor"),
            P("pipe", "shard", "tensor"),
            P("pipe", "shard"),
            P("pipe", "shard", "tensor"),
            P("pipe", "shard"),
            P("pipe", "shard"),
            P("pipe", "shard"),
            P("pipe", "shard"),
            P("pipe", "shard"),
        ),
        check_vma=False,
    )
```

profile of v0, /device:TPU:0, one launch (start us, length us, event | category | flops | bytes accessed | tf_op | source)
XLA Modules:
  0.0 1766.5 jit_solution(893844483868518288)
XLA Ops:
  8.8 25.5 %all-gather.3 = bf16[1,64,6]{2,0,1:T(2,128)(2,1)S(1)} all-gather(bf16[1,2,6]{2,0,1:T(2,128)(2,1)S(1)} %copy.203), channel_id=5, replica_groups=mesh['pipe'=2,'shard'=32,'tensor'=2] {'shard'}, dimensions={1}, use_global_device_ids=true | all-gather | bytes 792 | tf_op jit(solution)/shard_map/all_gather | solution.py:369
  34.6 24.2 %all-gather.2 = bf16[1,768,384]{2,1,0:T(8,128)(2,1)S(1)} all-gather(bf16[1,24,384]{2,1,0:T(8,128)(2,1)} %param.23), channel_id=4, replica_groups=mesh['pipe'=2,'shard'=32,'tensor'=2] {'shard'}, dimensions={1}, use_global_device_ids=true | all-gather | bytes 608256 | tf_op jit(solution)/shard_map/all_gather | solution.py:369
  65.7 126.4 %all-reduce.20 = (bf16[768]{0:T(1024)(128)(2,1)S(1)}, bf16[768]{0:T(1024)(128)(2,1)S(1)}, bf16[768]{0:T(1024)(128)(2,1)S(1)}, bf16[768]{0:T(1024)(128)(2,1)S(1)}...) all-reduce(bf16[768]{0:T(1024)(128)(2,1)S(1)} %dynamic-update-slice, ...), channel_id=3, replica_groups=mesh['pipe'=2,'shard'=32,'tensor'=2] {'shard'}, use_global_device_ids=true, to_apply=%add.1 | all-reduce | flops 4608 | bytes 18432
  216.1 25.6 %all-gather.4 = bf16[1,768,384]{2,1,0:T(8,128)(2,1)S(1)} all-gather(bf16[1,24,384]{2,1,0:T(8,128)(2,1)S(1)} %copy-done.182), channel_id=6, replica_groups=mesh['pipe'=2,'shard'=32,'tensor'=2] {'shard'}, dimensions={1}, use_global_device_ids=true | all-gather | bytes 608256 | tf_op jit(solution)/shard_map/all_gather | solution.py:369
  268.9 25.1 %all-gather.7 = bf16[1,768,384]{2,1,0:T(8,128)(2,1)S(1)} all-gather(bf16[1,24,384]{2,1,0:T(8,128)(2,1)} %param.24), channel_id=9, replica_groups=mesh['pipe'=2,'shard'=32,'tensor'=2] {'shard'}, dimensions={1}, use_global_device_ids=true | all-gather | bytes 608256 | tf_op jit(solution)/shard_map/all_gather | solution.py:369
  350.1 39.9 %all-gather.20.cloned.1.call-done = bf16[1,768,1536]{2,1,0:T(8,128)(2,1)} async-done(((bf16[1,24,1536]{2,1,0:T(8,128)(2,1)}), bf16[1,768,1536]{2,1,0:T(8,128)(2,1)}) %all-gather.20.cloned.1.call-update) | async-done | bytes 2359312 | tf_op jit(solution)/shard_map/all_gather | solution.py:369
  400.7 30.5 %all-reduce.44.cloned.1.call-done = f32[192,768]{1,0:T(8,128)} async-done(((f32[192,768]{1,0:T(8,128)}), f32[192,768]{1,0:T(8,128)}) %all-reduce.44.cloned.1.call-update) | async-done | bytes 589840 | tf_op jit(solution)/shard_map/psum | solution.py:193
  462.8 37.2 %all-reduce.46.cloned.1.call-done = f32[192,768]{1,0:T(8,128)} async-done(((f32[192,768]{1,0:T(8,128)}), f32[192,768]{1,0:T(8,128)}) %all-reduce.46.cloned.1.call-update) | async-done | bytes 589840 | tf_op jit(solution)/shard_map/psum | solution.py:187
  513.1 32.5 %all-reduce.48.cloned.1.call-done = f32[192,768]{1,0:T(8,128)} async-done(((f32[192,768]{1,0:T(8,128)}), f32[192,768]{1,0:T(8,128)}) %all-reduce.48.cloned.1.call-update) | async-done | bytes 589840 | tf_op jit(solution)/shard_map/psum | solution.py:193
  577.1 35.9 %all-reduce.50.cloned.1.call-done = f32[192,768]{1,0:T(8,128)} async-done(((f32[192,768]{1,0:T(8,128)}), f32[192,768]{1,0:T(8,128)}) %all-reduce.50.cloned.1.call-update) | async-done | bytes 589840 | tf_op jit(solution)/shard_map/psum | solution.py:187
  625.6 33.0 %all-reduce.52.cloned.1.call-done = f32[192,768]{1,0:T(8,128)} async-done(((f32[192,768]{1,0:T(8,128)}), f32[192,768]{1,0:T(8,128)}) %all-reduce.52.cloned.1.call-update) | async-done | bytes 589840 | tf_op jit(solution)/shard_map/psum | solution.py:193
  690.4 35.4 %all-reduce.54.cloned.1.call-done = f32[192,768]{1,0:T(8,128)} async-done(((f32[192,768]{1,0:T(8,128)}), f32[192,768]{1,0:T(8,128)}) %all-reduce.54.cloned.1.call-update) | async-done | bytes 589840 | tf_op jit(solution)/shard_map/psum | solution.py:187
  737.4 34.0 %all-reduce.56.cloned.1.call-done = f32[192,768]{1,0:T(8,128)} async-done(((f32[192,768]{1,0:T(8,128)}), f32[192,768]{1,0:T(8,128)}) %all-reduce.56.cloned.1.call-update) | async-done | bytes 589840 | tf_op jit(solution)/shard_map/psum | solution.py:193
  815.3 23.3 %all-reduce.58.cloned.1.call-done = f32[192,768]{1,0:T(8,128)} async-done(((f32[192,768]{1,0:T(8,128)}), f32[192,768]{1,0:T(8,128)}) %all-reduce.58.cloned.1.call-update) | async-done | bytes 589840 | tf_op jit(solution)/shard_map/psum | solution.py:187
  856.3 26.2 %all-reduce.62.cloned.1.call-done = bf16[192,768]{1,0:T(8,128)(2,1)} async-done(((bf16[192,768]{1,0:T(8,128)(2,1)}), bf16[192,768]{1,0:T(8,128)(2,1)}) %all-reduce.62.cloned.1.call-update) | async-done | bytes 294928 | tf_op jit(solution)/shard_map/psum | solution.py:253
  901.2 27.2 %all-reduce.64.cloned.1.call-done = bf16[192,768]{1,0:T(8,128)(2,1)} async-done(((bf16[192,768]{1,0:T(8,128)(2,1)}), bf16[192,768]{1,0:T(8,128)(2,1)}) %all-reduce.64.cloned.1.call-update) | async-done | bytes 294928 | tf_op jit(solution)/shard_map/psum | solution.py:279
  996.8 27.3 %all-reduce.68.cloned.1.call-done = bf16[192,768]{1,0:T(8,128)(2,1)} async-done(((bf16[192,768]{1,0:T(8,128)(2,1)}), bf16[192,768]{1,0:T(8,128)(2,1)}) %all-reduce.68.cloned.1.call-update) | async-done | bytes 294928 | tf_op jit(solution)/shard_map/psum | solution.py:279
  1093.1 27.6 %all-reduce.72.cloned.1.call-done = bf16[192,768]{1,0:T(8,128)(2,1)} async-done(((bf16[192,768]{1,0:T(8,128)(2,1)}), bf16[192,768]{1,0:T(8,128)(2,1)}) %all-reduce.72.cloned.1.call-update) | async-done | bytes 294928 | tf_op jit(solution)/shard_map/psum | solution.py:279
  1192.3 25.9 %all-reduce.76.cloned.1.call-done = bf16[192,768]{1,0:T(8,128)(2,1)} async-done(((bf16[192,768]{1,0:T(8,128)(2,1)}), bf16[192,768]{1,0:T(8,128)(2,1)}) %all-reduce.76.cloned.1.call-update) | async-done | bytes 294928 | tf_op jit(solution)/shard_map/psum | solution.py:279
  1348.9 128.3 %all-reduce.19 = (bf16[64,6]{1,0:T(8,128)(2,1)S(1)}, bf16[64,6]{1,0:T(8,128)(2,1)S(1)}, bf16[768]{0:T(1024)(128)(2,1)S(1)}, bf16[64,24]{0,1:T(8,128)(2,1)S(1)}, ...) all-reduce(bf16[64,6]{1,0:T(8,128)(2,1)S(1)} %copy.264, ...), channel_id=23, replica_groups=mesh['pipe'=2,'shard'=32,'tensor'=2] {'shard'}, use_global_device_ids=true, to_apply=%region_86.87.clone | all-reduce | flops 6912 | bytes 27648
  1487.8 26.9 %reduce-scatter.24.cloned.1.call-done = bf16[24,384]{1,0:T(8,128)(2,1)} async-done(((bf16[768,384]{1,0:T(8,128)(2,1)}), bf16[24,384]{1,0:T(8,128)(2,1)}) %reduce-scatter.24.cloned.1.call-update) | async-done | bytes 18448
  1516.0 76.5 %reduce-scatter.26.cloned.1.call-done = bf16[24,384]{1,0:T(8,128)(2,1)} async-done(((bf16[768,384]{1,0:T(8,128)(2,1)}), bf16[24,384]{1,0:T(8,128)(2,1)}) %reduce-scatter.26.cloned.1.call-update) | async-done | bytes 18448
  1593.9 80.7 %reduce-scatter.16.cloned.1.call-done = bf16[24,1536]{1,0:T(8,128)(2,1)} async-done(((bf16[768,1536]{1,0:T(8,128)(2,1)}), bf16[24,1536]{1,0:T(8,128)(2,1)}) %reduce-scatter.16.cloned.1.call-update) | async-done | bytes 73744 | tf_op jit(solution)/shard_map/reduce_scatter | solution.py:423
  1676.2 81.0 %reduce-scatter.18.cloned.1.call-done = bf16[24,1536]{1,0:T(8,128)(2,1)} async-done(((bf16[768,1536]{1,0:T(8,128)(2,1)}), bf16[24,1536]{1,0:T(8,128)(2,1)}) %reduce-scatter.18.cloned.1.call-update) | async-done | bytes 73744 | tf_op jit(solution)/shard_map/reduce_scatter | solution.py:423
  (996 shorter events, 689.3 us)
Async XLA Ops:
  8.0 327.0 %all-reduce.42.cloned.1.call-start = ((), (), s32[]{:S(2)}) async-start(), calls=%async_computation.6 | async-start | bytes 1179648 | tf_op jit(solution)/shard_map/psum | solution.py:187
  298.7 91.3 %all-gather.20.cloned.1.call-start = ((), (), s32[]{:S(2)}) async-start(), calls=%async_computation.29 | async-start | bytes 2433024 | tf_op jit(solution)/shard_map/all_gather | solution.py:369
  299.3 131.8 %all-reduce.44.cloned.1.call-start = ((), (), s32[]{:S(2)}) async-start(), calls=%async_computation.7 | async-start | bytes 1179648 | tf_op jit(solution)/shard_map/psum | solution.py:193
  393.6 106.4 %all-reduce.46.cloned.1.call-start = ((), (), s32[]{:S(2)}) async-start(), calls=%async_computation.8 | async-start | bytes 1179648 | tf_op jit(solution)/shard_map/psum | solution.py:187
  460.5 85.1 %all-reduce.48.cloned.1.call-start = ((), (), s32[]{:S(2)}) async-start(), calls=%async_computation.9 | async-start | bytes 1179648 | tf_op jit(solution)/shard_map/psum | solution.py:193
  508.0 105.0 %all-reduce.50.cloned.1.call-start = ((), (), s32[]{:S(2)}) async-start(), calls=%async_computation.10 | async-start | bytes 1179648 | tf_op jit(solution)/shard_map/psum | solution.py:187
  573.4 85.2 %all-reduce.52.cloned.1.call-start = ((), (), s32[]{:S(2)}) async-start(), calls=%async_computation.11 | async-start | bytes 1179648 | tf_op jit(solution)/shard_map/psum | solution.py:193
  620.9 104.9 %all-reduce.54.cloned.1.call-start = ((), (), s32[]{:S(2)}) async-start(), calls=%async_computation.12 | async-start | bytes 1179648 | tf_op jit(solution)/shard_map/psum | solution.py:187
  686.2 85.2 %all-reduce.56.cloned.1.call-start = ((), (), s32[]{:S(2)}) async-start(), calls=%async_computation.13 | async-start | bytes 1179648 | tf_op jit(solution)/shard_map/psum | solution.py:193
  733.7 104.9 %all-reduce.58.cloned.1.call-start = ((), (), s32[]{:S(2)}) async-start(), calls=%async_computation.14 | async-start | bytes 1179648 | tf_op jit(solution)/shard_map/psum | solution.py:187
  799.1 83.4 %all-reduce.62.cloned.1.call-start = ((), (), s32[]{:S(2)}) async-start(), calls=%async_computation.16 | async-start | bytes 589824 | tf_op jit(solution)/shard_map/psum | solution.py:253
  897.1 81.0 %all-reduce.66.cloned.1.call-start = ((), (), s32[]{:S(2)}) async-start(), calls=%async_computation.18 | async-start | bytes 589824 | tf_op jit(solution)/shard_map/psum | solution.py:253
  992.8 81.9 %all-reduce.70.cloned.1.call-start = ((), (), s32[]{:S(2)}) async-start(), calls=%async_computation.20 | async-start | bytes 589824 | tf_op jit(solution)/shard_map/psum | solution.py:253
  1089.4 82.3 %all-reduce.74.cloned.1.call-start = ((), (), s32[]{:S(2)}) async-start(), calls=%async_computation.22 | async-start | bytes 589824 | tf_op jit(solution)/shard_map/psum | solution.py:253
  1141.0 77.2 %all-reduce.76.cloned.1.call-start = ((), (), s32[]{:S(2)}) async-start(), calls=%async_computation.23 | async-start | bytes 589824 | tf_op jit(solution)/shard_map/psum | solution.py:279
  1187.0 81.8 %all-reduce.78.cloned.1.call-start = ((), (), s32[]{:S(2)}) async-start(), calls=%async_computation.24 | async-start | bytes 589824 | tf_op jit(solution)/shard_map/psum | solution.py:253
  1238.1 85.8 %all-reduce.60.cloned.1.call-start = ((), (), s32[]{:S(2)}) async-start(), calls=%async_computation.15 | async-start | bytes 1179648 | tf_op jit(solution)/shard_map/psum | solution.py:193
  1240.9 106.3 %all-reduce.80.cloned.1.call-start = ((), (), s32[]{:S(2)}) async-start(), calls=%async_computation.25 | async-start | bytes 589824 | tf_op jit(solution)/shard_map/psum | solution.py:279
  1280.3 204.8 %reduce-scatter.20.cloned.1.call-start = ((), (), s32[]{:S(2)}) async-start(), calls=%async_computation.30 | async-start | bytes 608256
  1284.3 202.2 %reduce-scatter.22.cloned.1.call-start = ((), (), s32[]{:S(2)}) async-start(), calls=%async_computation.31 | async-start | bytes 608256
  1293.6 221.0 %reduce-scatter.24.cloned.1.call-start = ((), (), s32[]{:S(2)}) async-start(), calls=%async_computation.32 | async-start | bytes 608256
  1300.7 291.9 %reduce-scatter.26.cloned.1.call-start = ((), (), s32[]{:S(2)}) async-start(), calls=%async_computation.33 | async-start | bytes 608256
  1308.3 366.3 %reduce-scatter.16.cloned.1.call-start = ((), (), s32[]{:S(2)}) async-start(), calls=%async_computation.26 | async-start | bytes 2433024 | tf_op jit(solution)/shard_map/reduce_scatter | solution.py:423
  1317.6 439.5 %reduce-scatter.18.cloned.1.call-start = ((), (), s32[]{:S(2)}) async-start(), calls=%async_computation.27 | async-start | bytes 2433024 | tf_op jit(solution)/shard_map/reduce_scatter | solution.py:423
  (279 other events, 2916.6 us)
Sparse Core Ops, SparseCore 0:
  298.3 36.6 all-reduce.41
  393.8 37.3 all-reduce.43
  460.6 39.3 all-reduce.45
  508.1 37.5 all-reduce.47
  573.5 39.3 all-reduce.49
  621.0 37.5 all-reduce.51
  686.3 39.4 all-reduce.53
  733.9 37.5 all-reduce.55
  799.2 39.4 all-reduce.57
  851.4 31.1 all-reduce.61
  897.2 31.1 all-reduce.63
  947.5 30.5 all-reduce.65
  992.9 31.1 all-reduce.67
  1044.1 30.5 all-reduce.69
  1089.6 31.1 all-reduce.71
  1141.2 30.5 all-reduce.73
  1187.1 31.1 all-reduce.75
  1238.2 30.5 all-reduce.77
  1271.4 37.5 all-reduce.59
  1311.2 31.1 all-reduce.79
Sparse Core Ops, SparseCore 1:
  301.1 42.8 all-gather.17
  346.4 43.5 all-gather.19
  1284.3 74.4 reduce-scatter.19
  1362.4 74.3 reduce-scatter.21
  1440.2 74.4 reduce-scatter.23
  1518.2 74.3 reduce-scatter.25
  1596.0 78.6 reduce-scatter.15
  1678.5 78.6 reduce-scatter.17
where the time goes:
time: 1780 us; the launch traced here: 1770 us
  waiting for transfers between devices  828 us (47%)
  blocking collectives  419 us (24%)
  matrix products  225 us (13%)
  other arithmetic  131 us (7%)
  local copies, waits for them, and re-layouts  123 us (7%)
  between operations  21.1 us (1%)
  starting transfers between devices  18.2 us (1%)
    unnamed x2, blocking collectives  255 us
    all_gather x7, blocking collectives, local(): lax.all_gather(shortened(local_params), 'shard', axis=0, tiled=True)  165 us
    reduce_scatter x2, waiting for transfers between devices, local(): lax.psum_scatter(shortened(arrange(totals)), 'shard', scatter_dimension=0...  162 us
    psum x5, waiting for transfers between devices, layer_forward(): head_total = lax.psum(contract_cols(mixed_b, w_out), 'tensor')  140 us
    psum x5, waiting for transfers between devices, layer_forward(): unit_total = lax.psum(contract_cols(active_b, w_down), 'tensor')  130 us
    psum x5, waiting for transfers between devices, layer_backward(): lax.psum(partial_normed.astype(jnp.bfloat16), 'tensor').astype(jnp.float32)  108 us
    unnamed x32, waiting for transfers between devices  105 us
    psum x5, waiting for transfers between devices, layer_backward(): lax.psum(contract_cols(grad_upper_b, w_up).astype(jnp.bfloat16), 'tensor')  96.1 us
  transfers between devices with their start and end apart: 36, of which 32 were waited for; matrix products, arithmetic and copies ran while one was open for 14% of the time, Pallas kernels for 0%

commit v1 on v0

v1 whole, which is shorter than its diff:
```python
import jax
import jax.numpy as jnp
import numpy as np
from jax import lax
from jax.sharding import Mesh
from jax.sharding import PartitionSpec as P

HEAD = 64
bf16 = jnp.bfloat16
f32 = jnp.float32

half_root = 0.7071067811865476
gauss_factor = 0.3989422804014327


EXCHANGES = {"xu": ("x", 1), "xv": ("x", 3), "zu": ("z", 1), "zv": ("z", 3), "c": ("core", 1)}
SIZES = {"x": 4, "z": 4, "core": 2}
WEIGHT_BITS = ("c", "zv", "zu", "xv", "xu")
SHARD_MASK = {"c": 1, "xu": 2, "xv": 6, "zu": 8, "zv": 24}
ORDERS = (
    ("xu", "xv", "zu", "zv"),
    ("xv", "xu", "zv", "zu"),
    ("zu", "zv", "xu", "xv"),
    ("zv", "zu", "xv", "xu"),
)
MASKS = np.zeros(32, np.int32)
for _index in range(32):
    for _place, _bit in enumerate(WEIGHT_BITS):
        if (_index >> (4 - _place)) & 1:
            MASKS[_index] ^= SHARD_MASK[_bit]


def exchange(value, bit):
    axis, flip = EXCHANGES[bit]
    return lax.ppermute(value, axis, [(i, i ^ flip) for i in range(SIZES[axis])])


def exchange_pipe(value):
    return lax.ppermute(value, "pipe", [(0, 1), (1, 0)])


def exchange_both(value):
    return lax.ppermute(value, ("pipe", "tensor"), [(i, i ^ 3) for i in range(4)])


def exchange_tensor(value):
    return lax.ppermute(value, "tensor", [(0, 1), (1, 0)])


def dot(left_side, right_side):
    return jnp.dot(left_side, right_side, preferred_element_type=f32)


def contract_rows(left_side, right_side):
    return lax.dot_general(left_side, right_side, (((0,), (0,)), ((), ())), preferred_element_type=f32)


def contract_cols(left_side, right_side):
    return lax.dot_general(left_side, right_side, (((1,), (1,)), ((), ())), preferred_element_type=f32)


def norm_forward(values, norm_gain, norm_shift):
    center = values - jnp.mean(values, -1, keepdims=True)
    rescale = lax.rsqrt(jnp.mean(center * center, -1, keepdims=True) + 1e-05)
    normed = center * rescale
    return (normed * norm_gain + norm_shift, normed, rescale)


def norm_backward(grad_rows, normed, rescale, norm_gain):
    scaled = grad_rows * norm_gain
    inner = (
        scaled
        - jnp.mean(scaled, -1, keepdims=True)
        - normed * jnp.mean(scaled * normed, -1, keepdims=True)
    )
    return (rescale * inner, jnp.sum(grad_rows * normed, 0), jnp.sum(grad_rows, 0))


def gelu_slope(pre_active):
    return (
        0.5 * (1.0 + lax.erf(pre_active * half_root))
        + pre_active * jnp.exp(-0.5 * pre_active * pre_active) * gauss_factor
    )


def pack_parts(w_query, w_key, w_value, w_out, w_up, w_down, small):
    return (
        jnp.concatenate([w_query, w_key, w_value], 1),
        jnp.concatenate([w_out, small, w_up[:, :768]], 1),
        jnp.concatenate([w_up[:, 768:], w_down[:, :384]], 1),
        w_down[:, 384:],
    )


def unpack_parts(parts):
    first, second, third, fourth = parts
    return (
        first[:, :384],
        first[:, 384:768],
        first[:, 768:],
        second[:, :384],
        jnp.concatenate([second[:, 512:], third[:, :768]], 1),
        jnp.concatenate([third[:, 768:], fourth], 1),
        second[:, 384:512],
    )


PART_COLS = (1152, 1280, 1152, 1152)
PART_ENDS = (0, 1152, 2432, 3584, 4736)


def split_parts(packed):
    return [packed[..., PART_ENDS[i] : PART_ENDS[i + 1]] for i in range(4)]


def gather_layers(own):
    pipe = lax.axis_index("pipe")
    other = exchange_pipe(own)
    mine = jnp.stack([jnp.where(pipe == 0, own, other), jnp.where(pipe == 0, other, own)])
    theirs = exchange_both(mine)
    parts = [
        jnp.concatenate([a, b], -1)[:, None] for a, b in zip(split_parts(mine), split_parts(theirs))
    ]
    for step in range(2):
        got = [exchange(part, ORDERS[i][step]) for i, part in enumerate(parts)]
        parts = [jnp.concatenate([a, b], 1) for a, b in zip(parts, got)]
    layers = []
    for layer in range(2):
        held = [part[layer] for part in parts]
        for step in range(2, 4):
            got = [exchange(part, ORDERS[i][step]) for i, part in enumerate(held)]
            held = [jnp.concatenate([a, b], 0) for a, b in zip(held, got)]
        got = [exchange(part, "c") for part in held]
        whole = []
        for i in range(4):
            both = jnp.stack([held[i], got[i]])
            axes = list(reversed(ORDERS[i]))
            cols = both.shape[-1]
            both = both.reshape((2, 2, 2, 2, 2, 24, cols))
            both = both.transpose([0] + [1 + axes.index(bit) for bit in WEIGHT_BITS[1:]] + [5, 6])
            whole.append(both.reshape(768, cols))
        layers.append(whole)
    return layers


def scatter_plane_large(parts):
    out = []
    for i, part in enumerate(parts):
        cols = part.shape[-1]
        out.append(part.reshape(2, 2, 2, 2, 2, 24, cols))
    got = [exchange(part[1], "c") for part in out]
    out = [add(part[0], other) for part, other in zip(out, got)]
    names = [list(WEIGHT_BITS[1:]) for _ in range(4)]
    return halve(out, names, (3, 2)), names


def add(left_side, right_side):
    return (left_side.astype(f32) + right_side.astype(f32)).astype(bf16)


def halve(parts, names, steps):
    for step in steps:
        keep, send = [], []
        for i, part in enumerate(parts):
            axis = names[i].index(ORDERS[i][step]) + part.ndim - 2 - len(names[i])
            keep.append(lax.index_in_dim(part, 0, axis, False))
            send.append(lax.index_in_dim(part, 1, axis, False))
        got = [exchange(part, ORDERS[i][step]) for i, part in enumerate(send)]
        for i in range(4):
            names[i].remove(ORDERS[i][step])
        parts = [add(a, b) for a, b in zip(keep, got)]
    return parts


def scatter_end(first_layer, second_layer, names):
    pipe = lax.axis_index("pipe")
    parts = [jnp.stack([a, b]) for a, b in zip(first_layer, second_layer)]
    parts = halve(parts, names, (1, 0))
    mine = jnp.concatenate([part[..., : PART_COLS[i]] for i, part in enumerate(parts)], -1)
    theirs = jnp.concatenate([part[..., PART_COLS[i] :] for i, part in enumerate(parts)], -1)
    total = mine.astype(f32) + exchange_both(theirs).astype(f32)
    keep = jnp.where(pipe == 0, total[0], total[1])
    send = jnp.where(pipe == 0, total[1], total[0]).astype(bf16)
    return keep + exchange_pipe(send).astype(f32)


def pack_small(b_query, b_value, b_up, vectors):
    rows = jnp.concatenate([b_query, b_value, b_up], 1)
    rows = jnp.pad(rows, ((0, 22), (0, 128 - 32 - 36)))
    cols = jnp.pad(jnp.stack(vectors, 1), ((0, 0), (0, 26)))
    return jnp.concatenate([cols, rows], 1)


def unpack_small(small):
    rows = small[:2, 32:68]
    return (rows[:, :6], rows[:, 6:12], rows[:, 12:36], [small[:, i] for i in range(6)])


def spread_small(small, place_units):
    vectors = [small[:, i].astype(f32) for i in range(6)]
    rows = jnp.concatenate([small[:, 32:68], small[:, 160:196]], 1)
    rows = rows.reshape(32, 24, 72)[:, :2].reshape(64, 72)
    rows = dot(place_units, rows)
    rows = rows.reshape(64, 2, 36)
    b_query = rows[:, :, :6].transpose(1, 2, 0).reshape(-1)
    b_value = rows[:, :, 6:12].transpose(1, 2, 0).reshape(-1)
    b_up = rows[:, :, 12:].transpose(1, 2, 0).reshape(-1)
    return b_query, b_value, b_up, vectors


def gather_small(b_query, b_value, b_up, vectors, place_units):
    rows = jnp.concatenate(
        [b_query.reshape(2, 6, HEAD), b_value.reshape(2, 6, HEAD), b_up.reshape(2, 24, HEAD)], 1
    )
    rows = rows.transpose(2, 0, 1).reshape(HEAD, 72).astype(bf16)
    rows = contract_rows(place_units, rows).astype(bf16)
    rows = jnp.pad(rows.reshape(32, 2, 72), ((0, 0), (0, 22), (0, 0))).reshape(768, 72)
    cols = jnp.pad(jnp.stack(vectors, 1).astype(bf16), ((0, 0), (0, 26)))
    gap = jnp.zeros((768, 60), bf16)
    return [jnp.concatenate([cols, rows[:, 36 * i : 36 * i + 36], gap], 1) for i in range(2)]


def layer_weights(whole, place_units):
    first, second, third, fourth = whole
    w_out = jnp.concatenate([second[:, :384], second[:, 1280:1664]], 1)
    small = jnp.concatenate([second[:, 384:512], second[:, 1664:1792]], 1)
    w_up = jnp.concatenate(
        [second[:, 512:1280], third[:, :768], second[:, 1792:], third[:, 1152:1920]], 1
    )
    w_down = jnp.concatenate(
        [third[:, 768:1152], fourth[:, :1152], third[:, 1920:], fourth[:, 1152:]], 1
    )
    b_query, b_value, b_up, vectors = spread_small(small, place_units)
    zeros = jnp.zeros((2, 384), f32)
    b_first = jnp.concatenate(
        [b_query.reshape(2, 384), zeros, b_value.reshape(2, 384)], 1
    ).reshape(-1)
    return (first, w_out, w_up, w_down, b_first, b_up, vectors)


def to_heads(rows):
    return rows.reshape(rows.shape[0], 2, 3, 6, HEAD).transpose(2, 1, 3, 0, 4).reshape(3, 12, -1, HEAD)


def layer_forward(section_in, length, weights):
    w_first, w_out, w_up, w_down, b_first, b_up, vectors = weights
    b_out, b_down, gain_one, shift_one, gain_two, shift_two = vectors
    normed, unit_one, scale_one = norm_forward(section_in, gain_one, shift_one)
    normed_b = normed.astype(bf16)
    heads = to_heads((dot(normed_b, w_first) + b_first).astype(bf16))
    query_b, key_b, value_b = heads[0], heads[1], heads[2]
    row_count = section_in.shape[0]
    scores = jnp.einsum("hqd,hkd->hqk", query_b, key_b, preferred_element_type=f32) * HEAD ** (-0.5)
    live_keys = (jnp.arange(row_count) < length)[None, None, :]
    scores = jnp.where(live_keys, scores, -1e30)
    powers = jnp.exp(scores - jnp.max(scores, -1, keepdims=True))
    soft = powers / jnp.sum(powers, -1, keepdims=True)
    soft_b = soft.astype(bf16)
    mixed = jnp.einsum("hqk,hkd->hqd", soft_b, value_b, preferred_element_type=f32)
    mixed_b = mixed.astype(bf16).transpose(1, 0, 2).reshape(row_count, -1)
    middle = section_in + contract_cols(mixed_b, w_out) + b_out
    normed_two, unit_two, scale_two = norm_forward(middle, gain_two, shift_two)
    normed_two_b = normed_two.astype(bf16)
    pre_active = dot(normed_two_b, w_up) + b_up
    active_b = jax.nn.gelu(pre_active, approximate=False).astype(bf16)
    result = middle + contract_cols(active_b, w_down) + b_down
    kept = (
        normed_b, unit_one, scale_one, query_b, key_b, value_b, soft, mixed_b,
        unit_two, scale_two, normed_two_b, pre_active, active_b,
    )
    return result, kept


def layer_backward(grad_rows, kept, weights, place_units):
    w_first, w_out, w_up, w_down, b_first, b_up, vectors = weights
    b_out, b_down, gain_one, shift_one, gain_two, shift_two = vectors
    (
        normed_b, unit_one, scale_one, query_b, key_b, value_b, soft, mixed_b,
        unit_two, scale_two, normed_two_b, pre_active, active_b,
    ) = kept
    row_count = grad_rows.shape[0]
    grad_b = grad_rows.astype(bf16)
    down_bias_term = jnp.sum(grad_rows, 0)
    down_term = contract_rows(grad_b, active_b).astype(bf16)
    grad_upper_b = (dot(grad_b, w_down) * gelu_slope(pre_active)).astype(bf16)
    up_bias_term = jnp.sum(grad_upper_b, 0, dtype=f32)
    up_term = contract_rows(normed_two_b, grad_upper_b).astype(bf16)
    grad_normed_two = contract_cols(grad_upper_b, w_up)
    grad_norm_two, gain_two_term, shift_two_term = norm_backward(
        grad_normed_two, unit_two, scale_two, gain_two
    )
    grad_middle = grad_rows + grad_norm_two
    out_bias_term = jnp.sum(grad_middle, 0)
    grad_middle_b = grad_middle.astype(bf16)
    out_term = contract_rows(grad_middle_b, mixed_b).astype(bf16)
    grad_mixed_b = dot(grad_middle_b, w_out).astype(bf16)
    grad_heads = grad_mixed_b.reshape(row_count, 12, HEAD).transpose(1, 0, 2)
    soft_b = soft.astype(bf16)
    grad_soft = jnp.einsum("hqd,hkd->hqk", grad_heads, value_b, preferred_element_type=f32)
    grad_scores_b = (soft * (grad_soft - jnp.sum(grad_soft * soft, -1, keepdims=True))).astype(bf16)
    factor = HEAD ** (-0.5)
    grad_query = jnp.einsum("hqk,hkd->hqd", grad_scores_b, key_b, preferred_element_type=f32) * factor
    grad_key = jnp.einsum("hqk,hqd->hkd", grad_scores_b, query_b, preferred_element_type=f32) * factor
    grad_value = jnp.einsum("hqk,hqd->hkd", soft_b, grad_heads, preferred_element_type=f32)
    grad_first_b = jnp.stack([grad_query.astype(bf16), grad_key.astype(bf16), grad_value.astype(bf16)])
    query_bias_term = jnp.sum(grad_first_b[0], 1, dtype=f32).reshape(-1)
    value_bias_term = jnp.sum(grad_first_b[2], 1, dtype=f32).reshape(-1)
    grad_first_b = (
        grad_first_b.reshape(3, 2, 6, row_count, HEAD).transpose(3, 1, 0, 2, 4).reshape(row_count, -1)
    )
    first_term = contract_rows(normed_b, grad_first_b).astype(bf16)
    grad_normed = contract_cols(grad_first_b, w_first)
    grad_norm_one, gain_one_term, shift_one_term = norm_backward(
        grad_normed, unit_one, scale_one, gain_one
    )
    grad_input = grad_middle + grad_norm_one
    small = gather_small(
        query_bias_term, value_bias_term, up_bias_term,
        [out_bias_term, down_bias_term, gain_one_term, shift_one_term, gain_two_term, shift_two_term],
        place_units,
    )
    parts = [
        first_term,
        jnp.concatenate(
            [out_term[:, :384], small[0], up_term[:, :768], out_term[:, 384:], small[1], up_term[:, 1536:2304]], 1
        ),
        jnp.concatenate(
            [up_term[:, 768:1536], down_term[:, :384], up_term[:, 2304:], down_term[:, 1536:1920]], 1
        ),
        jnp.concatenate([down_term[:, 384:1536], down_term[:, 1920:]], 1),
    ]
    return grad_input, parts


def share_outputs(first_rows, second_rows):
    pipe, tensor = lax.axis_index("pipe"), lax.axis_index("tensor")
    keep = jnp.where(pipe == 0, first_rows, second_rows)
    send = jnp.where(pipe == 0, second_rows, first_rows)
    same_pipe = exchange_tensor(keep)
    other_pipe = exchange_pipe(send)
    other_both = exchange_both(send)
    rows = jnp.stack([keep, same_pipe, other_pipe, other_both])
    rows = jnp.where(tensor == 0, rows, rows[jnp.array([1, 0, 3, 2])])
    return jnp.where(pipe == 0, rows, rows[jnp.array([2, 3, 0, 1])])[None]


def local(clip_frames, out_cotangent, clip_lengths, *params):
    params = [param[0] for param in params]
    w_query, w_key, w_value, w_out, w_up, w_down, b_query, b_value, b_out, b_up, b_down = params[:11]
    pipe, tensor = lax.axis_index("pipe"), lax.axis_index("tensor")
    shard = lax.axis_index("z") * 8 + lax.axis_index("x") * 2 + lax.axis_index("core")
    micro = pipe * 2 + tensor

    blocks = shard ^ jnp.asarray(MASKS)
    rows_at = (blocks[:, None] * 24 + jnp.arange(24)[None]).reshape(-1)
    place_rows = (jnp.arange(768)[:, None] == rows_at[None]).astype(bf16)
    units_at = (blocks[:, None] * 2 + jnp.arange(2)[None]).reshape(-1)
    place_units = (jnp.arange(64)[:, None] == units_at[None]).astype(bf16)

    small = pack_small(b_query, b_value, b_up, [b_out, b_down] + params[11:])
    own = jnp.concatenate(pack_parts(w_query, w_key, w_value, w_out, w_up, w_down, small), 1)
    layers = gather_layers(own)
    weights = [layer_weights(whole, place_units) for whole in layers]

    frames = lax.dynamic_index_in_dim(clip_frames, micro, 0, keepdims=False)
    cotangent = lax.dynamic_index_in_dim(out_cotangent, micro, 0, keepdims=False)
    length = lax.dynamic_index_in_dim(clip_lengths, micro, 0, keepdims=False)[0]
    section_in = dot(frames, place_rows)
    grad_out = dot(cotangent, place_rows)

    def placed_back(rows):
        return contract_cols(rows, place_rows).astype(bf16)

    first_out, kept_first = layer_forward(section_in, length, weights[0])
    first_out = first_out.astype(bf16)
    second_out, kept_second = layer_forward(first_out.astype(f32), length, weights[1])
    second_out = second_out.astype(bf16)
    section_output = share_outputs(placed_back(first_out), placed_back(second_out))

    second_grad, second_parts = layer_backward(grad_out, kept_second, weights[1], place_units)
    second_grad = second_grad.astype(bf16)
    second_parts, names = scatter_plane_large(second_parts)
    first_grad, first_parts = layer_backward(second_grad.astype(f32), kept_first, weights[0], place_units)
    first_grad = first_grad.astype(bf16)
    first_parts, _ = scatter_plane_large(first_parts)
    input_grad = share_outputs(placed_back(first_grad), placed_back(second_grad))

    total = scatter_end(first_parts, second_parts, names)
    (g_query, g_key, g_value, g_out, g_up, g_down, g_small) = unpack_parts(split_parts(total))
    gb_query, gb_value, gb_up, vectors = unpack_small(g_small)
    grads = [g_query, g_key, g_value, g_out, g_up, g_down, gb_query, gb_value, vectors[0], gb_up] + vectors[1:]
    return (section_output, input_grad) + tuple(grad[None] for grad in grads)


def solution(mesh):
    fine = Mesh(
        mesh.devices.reshape(2, 4, 4, 2, 2), ("pipe", "z", "x", "core", "tensor")
    )
    shard = ("z", "x", "core")
    rows = P(None, shard, None)
    matrix = P("pipe", shard, "tensor")
    vector = P("pipe", shard)
    params = (matrix,) * 8 + (vector, matrix) + (vector,) * 5
    return jax.shard_map(
        local,
        mesh=fine,
        in_specs=(rows, rows, P(None, shard)) + params,
        out_specs=(P("pipe", None, shard, None),) * 2 + params,
        check_vma=False,
    )
```

time: 1780 us -> 606 us (0.34)
  waiting for transfers between devices: 828 us -> 219 us
  blocking collectives: 419 us -> 0 us
  matrix products: 225 us -> 98.5 us
  starting transfers between devices: 18.2 us -> 89.1 us
  other arithmetic: 131 us -> 60.8 us
    psum x20 -> x0, waiting for transfers between devices: 474 us -> none  [the longest x5 140 us: layer_forward(): head_total = lax.psum(contract_cols(mixed_b, w_out), 'tensor')]
    unnamed x2 -> x0, blocking collectives: 255 us -> none
    ppermute x8 -> x74, waiting for transfers between devices: 41.3 us -> 219 us  [the longest x64 195 us: exchange(): lax.ppermute(value, axis, [(i, i ^ flip) for i in range(SIZES[axis])])]
    all_gather x7 -> x0, blocking collectives: 165 us -> none  [local(): lax.all_gather(shortened(local_params), 'shard', axis=0, tiled=True)]
    reduce_scatter x2 -> x0, waiting for transfers between devices: 162 us -> none  [local(): lax.psum_scatter(shortened(arrange(totals)), 'shard', scatter_dimension=0...]
    unnamed x32 -> x0, waiting for transfers between devices: 105 us -> none
    ppermute x8 -> x74, starting transfers between devices: 15.8 us -> 89.1 us  [the longest x64 73.8 us: exchange(): lax.ppermute(value, axis, [(i, i ^ flip) for i in range(SIZES[axis])])]
    dot_general x30 -> x10, matrix products: 84.6 us -> 19 us  [contract_rows(): lax.dot_general(left_side, right_side, (((0,), (0,)), ((), ())), preferre...]
  transfers between devices with their start and end apart: 36 -> 74, of which waited for: 32 -> 32; matrix products, arithmetic and copies ran while one was open for 14% -> 34% of each run, Pallas kernels for 0% -> 0%
where the time goes in v1:
time: 606 us; the launch traced here: 596 us
  waiting for transfers between devices  219 us (36%)
  local copies, waits for them, and re-layouts  124 us (20%)
  matrix products  98.5 us (16%)
  starting transfers between devices  89.1 us (15%)
  other arithmetic  60.8 us (10%)
    ppermute x64, waiting for transfers between devices, exchange(): lax.ppermute(value, axis, [(i, i ^ flip) for i in range(SIZES[axis])])  195 us
    ppermute x64, starting transfers between devices, exchange(): lax.ppermute(value, axis, [(i, i ^ flip) for i in range(SIZES[axis])])  73.8 us
    dot_general x12, matrix products, dot(): return jnp.dot(left_side, right_side, preferred_element_type=f32)  36.2 us
    dot_general x11, matrix products, contract_cols(): lax.dot_general(left_side, right_side, (((1,), (1,)), ((), ())), preferre...  24 us
    dot_general x10, matrix products, contract_rows(): lax.dot_general(left_side, right_side, (((0,), (0,)), ((), ())), preferre...  19 us
    slice x6, local copies, waits for them, and re-layouts, scatter_plane_large(): got = [exchange(part[1], 'c') for part in out]  17 us
    unnamed x387, local copies, waits for them, and re-layouts  16.1 us
    convert_element_type x24, other arithmetic, add(): return (left_side.astype(f32) + right_side.astype(f32)).astype(bf16)  14.5 us
  transfers between devices with their start and end apart: 74, of which 32 were waited for; matrix products, arithmetic and copies ran while one was open for 34% of the time, Pallas kernels for 0%

profile of v1, /device:TPU:0, one launch (start us, length us, event | category | flops | bytes accessed | tf_op | source)
XLA Modules:
  0.0 595.6 jit_solution(7730402084286955995)
XLA Ops:
  17.3 10.9 %collective-permute-done.1 = bf16[2,24,4736]{2,1,0:T(8,128)(2,1)S(1)} collective-permute-done((bf16[2,24,4736]{2,1,0:T(8,128)(2,1)S(1)}, bf16[2,24,4736]{2,1,0:T(8,128)(2,1)S(1)}, u32[]{:S(2)}, u32[]{:S(2)}) %collective-permute-start.1) | collective-permute-done | bytes 454688 | tf_op jit(solution)/shard_map/ppermute | solution.py:43
  44.8 6.1 %collective-permute-done.8 = bf16[2,2,24,2304]{3,2,0,1:T(8,128)(2,1)S(1)} collective-permute-done((bf16[2,2,24,2304]{3,2,0,1:T(8,128)(2,1)S(1)}, bf16[2,2,24,2304]{3,2,0,1:T(8,128)(2,1)S(1)}, u32[]{:S(2)}, u32[]{:S(2)}) %collective-permute-start.8) | collective-permute-done | bytes 442400 | tf_op jit(solution)/shard_map/ppermute | solution.py:35
  57.1 15.7 %collective-permute-done.19 = bf16[4,24,2304]{2,1,0:T(8,128)(2,1)S(1)} collective-permute-done((bf16[4,24,2304]{2,1,0:T(8,128)(2,1)S(1)}, bf16[4,24,2304]{2,1,0:T(8,128)(2,1)S(1)}, u32[]{:S(2)}, u32[]{:S(2)}) %collective-permute-start.19) | collective-permute-done | bytes 442400 | tf_op jit(solution)/shard_map/ppermute | solution.py:35
  83.2 16.1 %collective-permute-done.22 = bf16[4,24,2560]{2,1,0:T(8,128)(2,1)S(1)} collective-permute-done((bf16[4,24,2560]{2,1,0:T(8,128)(2,1)S(1)}, bf16[4,24,2560]{2,1,0:T(8,128)(2,1)S(1)}, u32[]{:S(2)}, u32[]{:S(2)}) %collective-permute-start.22) | collective-permute-done | bytes 491552 | tf_op jit(solution)/shard_map/ppermute | solution.py:35
  105.0 12.0 %collective-permute-done.15 = bf16[8,24,2304]{2,1,0:T(8,128)(2,1)S(1)} collective-permute-done((bf16[8,24,2304]{2,1,0:T(8,128)(2,1)S(1)}, bf16[8,24,2304]{2,1,0:T(8,128)(2,1)S(1)}, u32[]{:S(2)}, u32[]{:S(2)}) %collective-permute-start.15) | collective-permute-done | bytes 884768 | tf_op jit(solution)/shard_map/ppermute | solution.py:35
  120.7 9.3 %collective-permute-done.32 = bf16[8,24,2304]{2,1,0:T(8,128)(2,1)S(1)} collective-permute-done((bf16[8,24,2304]{2,1,0:T(8,128)(2,1)S(1)}, bf16[8,24,2304]{2,1,0:T(8,128)(2,1)S(1)}, u32[]{:S(2)}, u32[]{:S(2)}) %collective-permute-start.32) | collective-permute-done | bytes 884768 | tf_op jit(solution)/shard_map/ppermute | solution.py:35
  134.8 6.9 %collective-permute-done.5 = bf16[8,24,2560]{2,1,0:T(8,128)(2,1)S(1)} collective-permute-done((bf16[8,24,2560]{2,1,0:T(8,128)(2,1)S(1)}, bf16[8,24,2560]{2,1,0:T(8,128)(2,1)S(1)}, u32[]{:S(2)}, u32[]{:S(2)}) %collective-permute-start.5) | collective-permute-done | bytes 983072 | tf_op jit(solution)/shard_map/ppermute | solution.py:35
  141.9 13.2 %collective-permute-done.23 = bf16[8,24,2560]{2,1,0:T(8,128)(2,1)S(1)} collective-permute-done((bf16[8,24,2560]{2,1,0:T(8,128)(2,1)S(1)}, bf16[8,24,2560]{2,1,0:T(8,128)(2,1)S(1)}, u32[]{:S(2)}, u32[]{:S(2)}) %collective-permute-start.23) | collective-permute-done | bytes 983072 | tf_op jit(solution)/shard_map/ppermute | solution.py:35
  209.0 7.1 %fusion.16 = (bf16[192,3072]{1,0:T(8,128)(2,1)S(1)}, f32[192,3072]{1,0:T(8,128)}) fusion(f32[3072]{0:T(1024)S(1)} %add.378, bf16[768,768]{1,0:T(8,128)(2,1)S(1)} %copy-done.77, bf16[768,768]{1,0:T(8,128)(2,1)S(1)} %copy-done.75, bf16[768,768]{1,0:T(8,128)(2,1)S(1)} %copy-done.79, bf16[768,768]{1,0:T(8,128)(2,1)S(1)} %copy-done.73, ...), kind=kOutput, calls=%fused_computation.62 | convolution fusion | flops 964509696 | bytes 8867328 | tf_op jit(solution)/shard_map/dot_general | solution.py:51
  227.3 9.7 %fusion.19 = (bf16[192,3072]{1,0:T(8,128)(2,1)}, f32[192,3072]{1,0:T(8,128)}) fusion(f32[3072]{0:T(1024)S(1)} %add.396, bf16[768,768]{1,0:T(8,128)(2,1)S(1)} %copy-done.85, bf16[768,768]{1,0:T(8,128)(2,1)S(1)} %copy-done.83, bf16[768,768]{1,0:T(8,128)(2,1)S(1)} %copy-done.87, bf16[768,768]{1,0:T(8,128)(2,1)S(1)} %copy-done.81, ...), kind=kOutput, calls=%fused_computation.65 | convolution fusion | flops 964509696 | bytes 8867328 | tf_op jit(solution)/shard_map/dot_general | solution.py:51
  237.0 5.5 fusion.71
  247.2 6.4 %fusion.258 = (bf16[3072]{0:T(1024)(128)(2,1)}, bf16[192,3072]{1,0:T(8,128)(2,1)S(1)}) fusion(f32[192,3072]{1,0:T(8,128)} %get-tuple-element.191, bf16[768,1152]{1,0:T(8,128)(2,1)} %get-tuple-element.104, bf16[768,384]{1,0:T(8,128)(2,1)S(1)} %copy-done.107, bf16[768,1152]{1,0:T(8,128)(2,1)} %get-tuple-element.103, bf16[768,384]{1,0:T(8,128)(2,1)S(1)} %copy-done.106, ...), kind=kOutput, calls=%fused_computation.572 | convolution fusion | flops 931476480 | bytes 8853504 | tf_op jit(solution)/shard_map/dot_general | solution.py:51
  270.7 4.9 fusion.261
  339.6 6.7 %concatenate.234 = bf16[768,2560]{1,0:T(8,128)(2,1)} concatenate(bf16[768,384]{1,0:T(8,128)(2,1)} %copy.209, bf16[768,32]{1,0:T(8,128)(2,1)S(1)} %pad.24, bf16[768,36]{1,0:T(8,128)(2,1)} %get-tuple-element.165, bf16[768,60]{1,0:T(8,128)(2,1)S(1)} %broadcast.340, bf16[768,768]{1,0:T(8,128)(2,1)S(1)} %get-tuple-element.60, bf16[768,384]{1,0:T(8,128)(2,1)} %copy.210, ...), dimensions={1} | concatenate | bytes 7864320 | tf_op jit(solution)/shard_map/concatenate | solution.py:324
  354.7 7.6 %concatenate.236 = bf16[768,2560]{1,0:T(8,128)(2,1)} concatenate(bf16[768,384]{1,0:T(8,128)(2,1)} %copy.214, bf16[768,32]{1,0:T(8,128)(2,1)S(1)} %pad.26, bf16[768,36]{1,0:T(8,128)(2,1)S(1)} %copy-done.97, bf16[768,60]{1,0:T(8,128)(2,1)S(1)} %broadcast.340, bf16[768,768]{1,0:T(8,128)(2,1)} %get-tuple-element.64, bf16[768,384]{1,0:T(8,128)(2,1)S(1)} %copy.215, ...), dimensions={1} | concatenate | bytes 7864320 | tf_op jit(solution)/shard_map/concatenate | solution.py:324
  399.1 5.6 collective-permute-done.37
  431.3 8.8 %collective-permute-done.41 = bf16[2,2,2,24,2304]{4,3,2,1,0:T(8,128)(2,1)S(1)} collective-permute-done((bf16[2,2,2,24,2304]{4,3,2,1,0:T(8,128)(2,1)S(1)}, bf16[2,2,2,24,2304]{4,3,2,1,0:T(8,128)(2,1)S(1)}, u32[]{:S(2)}, u32[]{:S(2)}) %collective-permute-start.41) | collective-permute-done | bytes 884768 | tf_op jit(solution)/shard_map/ppermute | solution.py:35
  443.1 15.7 %collective-permute-done.44 = bf16[2,2,2,24,2304]{4,3,2,1,0:T(8,128)(2,1)S(1)} collective-permute-done((bf16[2,2,2,24,2304]{4,3,2,1,0:T(8,128)(2,1)S(1)}, bf16[2,2,2,24,2304]{4,3,2,1,0:T(8,128)(2,1)S(1)}, u32[]{:S(2)}, u32[]{:S(2)}) %collective-permute-start.44) | collective-permute-done | bytes 884768 | tf_op jit(solution)/shard_map/ppermute | solution.py:35
  468.4 15.0 %collective-permute-done.49 = bf16[2,2,2,24,2560]{4,3,1,2,0:T(8,128)(2,1)S(1)} collective-permute-done((bf16[2,2,2,24,2560]{4,3,1,2,0:T(8,128)(2,1)S(1)}, bf16[2,2,2,24,2560]{4,3,1,2,0:T(8,128)(2,1)S(1)}, u32[]{:S(2)}, u32[]{:S(2)}) %collective-permute-start.49) | collective-permute-done | bytes 983072 | tf_op jit(solution)/shard_map/ppermute | solution.py:35
  483.7 20.8 %collective-permute-done.52 = bf16[2,2,2,24,2560]{4,3,1,2,0:T(8,128)(2,1)S(1)} collective-permute-done((bf16[2,2,2,24,2560]{4,3,1,2,0:T(8,128)(2,1)S(1)}, bf16[2,2,2,24,2560]{4,3,1,2,0:T(8,128)(2,1)S(1)}, u32[]{:S(2)}, u32[]{:S(2)}) %collective-permute-start.52) | collective-permute-done | bytes 983072 | tf_op jit(solution)/shard_map/ppermute | solution.py:35
  507.7 6.2 %collective-permute-done.42 = bf16[2,2,24,2304]{3,2,1,0:T(8,128)(2,1)S(1)} collective-permute-done((bf16[2,2,24,2304]{3,2,1,0:T(8,128)(2,1)S(1)}, bf16[2,2,24,2304]{3,2,1,0:T(8,128)(2,1)S(1)}, u32[]{:S(2)}, u32[]{:S(2)}) %collective-permute-start.42) | collective-permute-done | bytes 442400 | tf_op jit(solution)/shard_map/ppermute | solution.py:35
  514.0 8.2 %collective-permute-done.45 = bf16[2,2,24,2304]{3,2,1,0:T(8,128)(2,1)S(1)} collective-permute-done((bf16[2,2,24,2304]{3,2,1,0:T(8,128)(2,1)S(1)}, bf16[2,2,24,2304]{3,2,1,0:T(8,128)(2,1)S(1)}, u32[]{:S(2)}, u32[]{:S(2)}) %collective-permute-start.45) | collective-permute-done | bytes 442400 | tf_op jit(solution)/shard_map/ppermute | solution.py:35
  532.0 5.6 collective-permute-done.50
  537.7 10.4 %collective-permute-done.53 = bf16[2,2,24,2560]{3,2,0,1:T(8,128)(2,1)S(1)} collective-permute-done((bf16[2,2,24,2560]{3,2,0,1:T(8,128)(2,1)S(1)}, bf16[2,2,24,2560]{3,2,0,1:T(8,128)(2,1)S(1)}, u32[]{:S(2)}, u32[]{:S(2)}) %collective-permute-start.53) | collective-permute-done | bytes 491552 | tf_op jit(solution)/shard_map/ppermute | solution.py:35
  (832 shorter events, 357.2 us)
Async XLA Ops:
  53.3 25.7 %collective-permute-start.28 = (bf16[4,24,2304]{2,1,0:T(8,128)(2,1)S(1)}, bf16[4,24,2304]{2,1,0:T(8,128)(2,1)S(1)}, u32[]{:S(2)}, u32[]{:S(2)}) collective-permute-start(bf16[4,24,2304]{2,1,0:T(8,128)(2,1)S(1)} %get-tuple-element.131), channel_id=1, source_target_pairs={{0,4},{4,0},{8,12},{12,8},{1,5},{5,1},{9,13},{13,9},{2,6},{6,2},{1... | collective-permute-start | bytes 1327112 | tf_op jit(solution)/shard_map/ppermute | solution.py:35
  73.3 28.2 %collective-permute-start.4 = (bf16[4,24,2560]{2,1,0:T(8,128)(2,1)S(1)}, bf16[4,24,2560]{2,1,0:T(8,128)(2,1)S(1)}, u32[]{:S(2)}, u32[]{:S(2)}) collective-permute-start(bf16[4,24,2560]{2,1,0:T(8,128)(2,1)S(1)} %get-tuple-element.127), channel_id=1, source_target_pairs={{0,48},{16,32},{32,16},{48,0},{1,49},{17,33},{33,17},{49,1},{2,50}... | collective-permute-start | bytes 1474568 | tf_op jit(solution)/shard_map/ppermute | solution.py:35
  76.9 55.9 %collective-permute-start.10 = (bf16[8,24,2304]{2,1,0:T(8,128)(2,1)S(1)}, bf16[8,24,2304]{2,1,0:T(8,128)(2,1)S(1)}, u32[]{:S(2)}, u32[]{:S(2)}) collective-permute-start(bf16[8,24,2304]{2,1,0:T(8,128)(2,1)S(1)} %pad_maximum_fusion.28), channel_id=1, source_target_pairs={{0,48},{16,32},{32,16},{48,0},{1,49},{17,33},{33,17},{49,1},{2,50}... | collective-permute-start | bytes 2654216 | tf_op jit(solution)/shard_map/ppermute | solution.py:35
  79.0 52.1 %collective-permute-start.26 = (bf16[8,24,2304]{2,1,0:T(8,128)(2,1)S(1)}, bf16[8,24,2304]{2,1,0:T(8,128)(2,1)S(1)}, u32[]{:S(2)}, u32[]{:S(2)}) collective-permute-start(bf16[8,24,2304]{2,1,0:T(8,128)(2,1)S(1)} %pad_maximum_fusion.33), channel_id=1, source_target_pairs={{0,48},{16,32},{32,16},{48,0},{1,49},{17,33},{33,17},{49,1},{2,50}... | collective-permute-start | bytes 2654216 | tf_op jit(solution)/shard_map/ppermute | solution.py:35
  120.5 34.6 %collective-permute-start.23 = (bf16[8,24,2560]{2,1,0:T(8,128)(2,1)S(1)}, bf16[8,24,2560]{2,1,0:T(8,128)(2,1)S(1)}, u32[]{:S(2)}, u32[]{:S(2)}) collective-permute-start(bf16[8,24,2560]{2,1,0:T(8,128)(2,1)S(1)} %pad_maximum_fusion.26), channel_id=1, source_target_pairs={{0,16},{16,0},{32,48},{48,32},{1,17},{17,1},{33,49},{49,33},{2,18}... | collective-permute-start | bytes 2949128 | tf_op jit(solution)/shard_map/ppermute | solution.py:35
  131.1 25.4 %collective-permute-start.33 = (bf16[16,24,2304]{2,1,0:T(8,128)(2,1)S(1)}, bf16[16,24,2304]{2,1,0:T(8,128)(2,1)S(1)}, u32[]{:S(2)}, u32[]{:S(2)}) collective-permute-start(bf16[16,24,2304]{2,1,0:T(8,128)(2,1)S(1)} %pad_maximum_fusion.17), channel_id=1, source_target_pairs={{0,2},{2,0},{1,3},{3,1},{4,6},{6,4},{5,7},{7,5},{8,10},{10,8},{9,1... | collective-permute-start | bytes 5308424 | tf_op jit(solution)/shard_map/ppermute | solution.py:35
  157.2 28.3 %collective-permute-start.6 = (bf16[16,24,2560]{2,1,0:T(8,128)(2,1)S(1)}, bf16[16,24,2560]{2,1,0:T(8,128)(2,1)}, u32[]{:S(2)}, u32[]{:S(2)}) collective-permute-start(bf16[16,24,2560]{2,1,0:T(8,128)(2,1)S(1)} %pad_maximum_fusion.8), channel_id=1, source_target_pairs={{0,2},{2,0},{1,3},{3,1},{4,6},{6,4},{5,7},{7,5},{8,10},{10,8},{9,1... | collective-permute-start | bytes 5898248 | tf_op jit(solution)/shard_map/ppermute | solution.py:35
  245.0 141.8 %collective-permute-start.36 = (bf16[192,768]{1,0:T(8,128)(2,1)}, bf16[192,768]{1,0:T(8,128)(2,1)}, u32[]{:S(2)}, u32[]{:S(2)}) collective-permute-start(bf16[192,768]{1,0:T(8,128)(2,1)} %get-tuple-element.139), channel_id=1, source_target_pairs={{0,65},{1,64},{64,1},{65,0},{2,67},{3,66},{66,3},{67,2},{4,69},{5,... | collective-permute-start | bytes 884744 | tf_op jit(solution)/shard_map/ppermute | solution.py:43
  247.1 141.8 %collective-permute-start.35 = (bf16[192,768]{1,0:T(8,128)(2,1)}, bf16[192,768]{1,0:T(8,128)(2,1)}, u32[]{:S(2)}, u32[]{:S(2)}) collective-permute-start(bf16[192,768]{1,0:T(8,128)(2,1)} %get-tuple-element.139), channel_id=1, source_target_pairs={{0,64},{64,0},{1,65},{65,1},{2,66},{66,2},{3,67},{67,3},{4,68},{68... | collective-permute-start | bytes 884744 | tf_op jit(solution)/shard_map/ppermute | solution.py:39
  317.0 72.0 %collective-permute-start.34 = (bf16[192,768]{1,0:T(8,128)(2,1)}, bf16[192,768]{1,0:T(8,128)(2,1)}, u32[]{:S(2)}, u32[]{:S(2)}) collective-permute-start(bf16[192,768]{1,0:T(8,128)(2,1)} %get-tuple-element.138), channel_id=1, source_target_pairs={{0,1},{1,0},{2,3},{3,2},{4,5},{5,4},{6,7},{7,6},{8,9},{9,8},{10,11... | collective-permute-start | bytes 884744 | tf_op jit(solution)/shard_map/ppermute | solution.py:47
  335.3 72.2 %collective-permute-start.40 = (bf16[2,2,2,2,24,2304]{5,4,3,2,1,0:T(8,128)(2,1)}, bf16[2,2,2,2,24,2304]{5,4,3,2,1,0:T(8,128)(2,1)}, u32[]{:S(2)}, u32[]{:S(2)}) collective-permute-start(bf16[2,2,2,2,24,2304]{5,4,3,2,1,0:T(8,128)(2,1)} %bitcast.135), channel_id=1, source_target_pairs={{0,2},{2,0},{1,3},{3,1},{4,6},{6,4},{5,7},{7,5},{8,10},{10,8},{9,1... | collective-permute-start | bytes 5308424 | tf_op jit(solution)/shard_map/ppermute | solution.py:35
  337.3 72.8 %collective-permute-start.43 = (bf16[2,2,2,2,24,2304]{5,4,3,2,1,0:T(8,128)(2,1)}, bf16[2,2,2,2,24,2304]{5,4,3,2,1,0:T(8,128)(2,1)}, u32[]{:S(2)}, u32[]{:S(2)}) collective-permute-start(bf16[2,2,2,2,24,2304]{5,4,3,2,1,0:T(8,128)(2,1)} %bitcast.143), channel_id=1, source_target_pairs={{0,2},{2,0},{1,3},{3,1},{4,6},{6,4},{5,7},{7,5},{8,10},{10,8},{9,1... | collective-permute-start | bytes 5308424 | tf_op jit(solution)/shard_map/ppermute | solution.py:35
  397.2 26.3 %collective-permute-start.48 = (bf16[2,2,2,2,24,2560]{5,4,2,3,0,1:T(8,128)(2,1)}, bf16[2,2,2,2,24,2560]{5,4,2,3,0,1:T(8,128)(2,1)}, u32[]{:S(2)}, u32[]{:S(2)}) collective-permute-start(bf16[2,2,2,2,24,2560]{5,4,2,3,0,1:T(8,128)(2,1)} %copy.211), channel_id=1, source_target_pairs={{0,2},{2,0},{1,3},{3,1},{4,6},{6,4},{5,7},{7,5},{8,10},{10,8},{9,1... | collective-permute-start | bytes 5898248 | tf_op jit(solution)/shard_map/ppermute | solution.py:35
  399.1 29.5 %collective-permute-start.51 = (bf16[2,2,2,2,24,2560]{5,4,2,3,0,1:T(8,128)(2,1)}, bf16[2,2,2,2,24,2560]{5,4,2,3,0,1:T(8,128)(2,1)}, u32[]{:S(2)}, u32[]{:S(2)}) collective-permute-start(bf16[2,2,2,2,24,2560]{5,4,2,3,0,1:T(8,128)(2,1)} %copy.216), channel_id=1, source_target_pairs={{0,2},{2,0},{1,3},{3,1},{4,6},{6,4},{5,7},{7,5},{8,10},{10,8},{9,1... | collective-permute-start | bytes 5898248 | tf_op jit(solution)/shard_map/ppermute | solution.py:35
  420.1 38.7 %collective-permute-start.44 = (bf16[2,2,2,24,2304]{4,3,2,1,0:T(8,128)(2,1)S(1)}, bf16[2,2,2,24,2304]{4,3,2,1,0:T(8,128)(2,1)S(1)}, u32[]{:S(2)}, u32[]{:S(2)}) collective-permute-start(bf16[2,2,2,24,2304]{4,3,2,1,0:T(8,128)(2,1)S(1)} %slice_bitcast_fusion.12), channel_id=1, source_target_pairs={{0,48},{16,32},{32,16},{48,0},{1,49},{17,33},{33,17},{49,1},{2,50}... | collective-permute-start | bytes 2654216 | tf_op jit(solution)/shard_map/ppermute | solution.py:35
  421.8 37.2 %collective-permute-start.68 = (bf16[2,2,2,24,2304]{4,3,0,1,2:T(8,128)(2,1)S(1)}, bf16[2,2,2,24,2304]{4,3,0,1,2:T(8,128)(2,1)S(1)}, u32[]{:S(2)}, u32[]{:S(2)}) collective-permute-start(bf16[2,2,2,24,2304]{4,3,0,1,2:T(8,128)(2,1)S(1)} %slice_bitcast_fusion.4), channel_id=1, source_target_pairs={{0,4},{4,0},{8,12},{12,8},{1,5},{5,1},{9,13},{13,9},{2,6},{6,2},{1... | collective-permute-start | bytes 2654216 | tf_op jit(solution)/shard_map/ppermute | solution.py:35
  423.5 37.9 %collective-permute-start.60 = (bf16[2,2,2,24,2304]{4,3,1,0,2:T(8,128)(2,1)S(1)}, bf16[2,2,2,24,2304]{4,3,1,0,2:T(8,128)(2,1)S(1)}, u32[]{:S(2)}, u32[]{:S(2)}) collective-permute-start(bf16[2,2,2,24,2304]{4,3,1,0,2:T(8,128)(2,1)S(1)} %slice_bitcast_fusion.8), channel_id=1, source_target_pairs={{0,12},{4,8},{8,4},{12,0},{1,13},{5,9},{9,5},{13,1},{2,14},{6,10},... | collective-permute-start | bytes 2654216 | tf_op jit(solution)/shard_map/ppermute | solution.py:35
  428.5 33.9 %collective-permute-start.65 = (bf16[2,2,2,24,2304]{4,3,0,1,2:T(8,128)(2,1)S(1)}, bf16[2,2,2,24,2304]{4,3,0,1,2:T(8,128)(2,1)S(1)}, u32[]{:S(2)}, u32[]{:S(2)}) collective-permute-start(bf16[2,2,2,24,2304]{4,3,0,1,2:T(8,128)(2,1)S(1)} %slice_bitcast_fusion.6), channel_id=1, source_target_pairs={{0,4},{4,0},{8,12},{12,8},{1,5},{5,1},{9,13},{13,9},{2,6},{6,2},{1... | collective-permute-start | bytes 2654216 | tf_op jit(solution)/shard_map/ppermute | solution.py:35
  459.0 45.4 %collective-permute-start.52 = (bf16[2,2,2,24,2560]{4,3,1,2,0:T(8,128)(2,1)S(1)}, bf16[2,2,2,24,2560]{4,3,1,2,0:T(8,128)(2,1)S(1)}, u32[]{:S(2)}, u32[]{:S(2)}) collective-permute-start(bf16[2,2,2,24,2560]{4,3,1,2,0:T(8,128)(2,1)S(1)} %slice_bitcast_fusion), channel_id=1, source_target_pairs={{0,16},{16,0},{32,48},{48,32},{1,17},{17,1},{33,49},{49,33},{2,18}... | collective-permute-start | bytes 2949128 | tf_op jit(solution)/shard_map/ppermute | solution.py:35
  461.4 52.6 %collective-permute-start.42 = (bf16[2,2,24,2304]{3,2,1,0:T(8,128)(2,1)S(1)}, bf16[2,2,24,2304]{3,2,1,0:T(8,128)(2,1)S(1)}, u32[]{:S(2)}, u32[]{:S(2)}) collective-permute-start(bf16[2,2,24,2304]{3,2,1,0:T(8,128)(2,1)S(1)} %slice_bitcast_fusion.32), channel_id=1, source_target_pairs={{0,16},{16,0},{32,48},{48,32},{1,17},{17,1},{33,49},{49,33},{2,18}... | collective-permute-start | bytes 1327112 | tf_op jit(solution)/shard_map/ppermute | solution.py:35
  462.4 59.8 %collective-permute-start.45 = (bf16[2,2,24,2304]{3,2,1,0:T(8,128)(2,1)S(1)}, bf16[2,2,24,2304]{3,2,1,0:T(8,128)(2,1)S(1)}, u32[]{:S(2)}, u32[]{:S(2)}) collective-permute-start(bf16[2,2,24,2304]{3,2,1,0:T(8,128)(2,1)S(1)} %slice_bitcast_fusion.30), channel_id=1, source_target_pairs={{0,16},{16,0},{32,48},{48,32},{1,17},{17,1},{33,49},{49,33},{2,18}... | collective-permute-start | bytes 1327112 | tf_op jit(solution)/shard_map/ppermute | solution.py:35
  465.3 59.7 %collective-permute-start.69 = (bf16[2,2,24,2304]{3,2,0,1:T(8,128)(2,1)S(1)}, bf16[2,2,24,2304]{3,2,0,1:T(8,128)(2,1)S(1)}, u32[]{:S(2)}, u32[]{:S(2)}) collective-permute-start(bf16[2,2,24,2304]{3,2,0,1:T(8,128)(2,1)S(1)} %slice_bitcast_fusion.22), channel_id=1, source_target_pairs={{0,12},{4,8},{8,4},{12,0},{1,13},{5,9},{9,5},{13,1},{2,14},{6,10},... | collective-permute-start | bytes 1327112 | tf_op jit(solution)/shard_map/ppermute | solution.py:35
  483.4 45.4 %collective-permute-start.61 = (bf16[2,2,24,2304]{3,2,1,0:T(8,128)(2,1)S(1)}, bf16[2,2,24,2304]{3,2,1,0:T(8,128)(2,1)S(1)}, u32[]{:S(2)}, u32[]{:S(2)}) collective-permute-start(bf16[2,2,24,2304]{3,2,1,0:T(8,128)(2,1)S(1)} %slice_bitcast_fusion.26), channel_id=1, source_target_pairs={{0,4},{4,0},{8,12},{12,8},{1,5},{5,1},{9,13},{13,9},{2,6},{6,2},{1... | collective-permute-start | bytes 1327112 | tf_op jit(solution)/shard_map/ppermute | solution.py:35
  529.2 28.4 %collective-permute-start.62 = (bf16[2,2,24,2304]{3,2,0,1:T(8,128)(2,1)S(1)}, bf16[2,2,24,2304]{3,2,0,1:T(8,128)(2,1)S(1)}, u32[]{:S(2)}, u32[]{:S(2)}) collective-permute-start(bf16[2,2,24,2304]{3,2,0,1:T(8,128)(2,1)S(1)} %fusion.140), channel_id=1, source_target_pairs={{0,48},{16,32},{32,16},{48,0},{1,49},{17,33},{33,17},{49,1},{2,50}... | collective-permute-start | bytes 1327112 | tf_op jit(solution)/shard_map/ppermute | solution.py:35
  (243 other events, 2678.0 us)

commit v2 on v1

v2 whole, which is shorter than its diff:
```python
import functools

import jax
import jax.numpy as jnp
import numpy as np
from jax import lax
from jax.experimental import pallas as pl
from jax.experimental.pallas import tpu as pltpu
from jax.sharding import Mesh
from jax.sharding import PartitionSpec as P

HEAD = 64
bf16 = jnp.bfloat16
f32 = jnp.float32

half_root = 0.7071067811865476
gauss_factor = 0.3989422804014327


def dot(left_side, right_side):
    return lax.dot_general(left_side, right_side, (((1,), (0,)), ((), ())), preferred_element_type=f32)


def dot_rows(left_side, right_side):
    return lax.dot_general(left_side, right_side, (((0,), (0,)), ((), ())), preferred_element_type=f32)


def dot_cols(left_side, right_side):
    return lax.dot_general(left_side, right_side, (((1,), (1,)), ((), ())), preferred_element_type=f32)


def norm_parts(values):
    center = values - jnp.mean(values, -1, keepdims=True)
    rescale = lax.rsqrt(jnp.mean(center * center, -1, keepdims=True) + 1e-05)
    return center * rescale, rescale


def norm_backward(grad_rows, normed, rescale, norm_gain):
    scaled = grad_rows * norm_gain
    inner = (
        scaled
        - jnp.mean(scaled, -1, keepdims=True)
        - normed * jnp.mean(scaled * normed, -1, keepdims=True)
    )
    return rescale * inner


def attention_forward_kernel(
    length_ref, x_ref, own_ref, peer_ref, own_out_ref, peer_out_ref, vec_ref,
    middle_ref, heads_ref, soft_ref, mixed_ref,
):
    length = length_ref[0]
    normed, _ = norm_parts(x_ref[...].astype(f32))
    normed_b = (normed * vec_ref[2:3] + vec_ref[3:4]).astype(bf16)
    for j in range(3):
        for half, weight_ref in enumerate((own_ref, peer_ref)):
            cols = slice(384 * half, 384 * half + 384)
            rows = dot(normed_b, weight_ref[j])
            if j != 1:
                rows = rows + vec_ref[6 + j // 2 : 7 + j // 2, cols]
            heads_ref[j, :, cols] = rows.astype(bf16)
    count = x_ref.shape[0]
    live_keys = lax.broadcasted_iota(jnp.int32, (count, count), 1) < length
    for pair in range(6):
        both = []
        for head in (2 * pair, 2 * pair + 1):
            cols = slice(HEAD * head, HEAD * head + HEAD)
            scores = dot_cols(heads_ref[0, :, cols], heads_ref[1, :, cols]) * HEAD ** (-0.5)
            scores = jnp.where(live_keys, scores, -1e30)
            powers = jnp.exp(scores - jnp.max(scores, -1, keepdims=True))
            soft = powers / jnp.sum(powers, -1, keepdims=True)
            soft_ref[head] = soft
            both.append(dot(soft.astype(bf16), heads_ref[2, :, cols]))
        mixed_ref[:, 128 * pair : 128 * pair + 128] = jnp.concatenate(both, 1).astype(bf16)
    total = dot_cols(mixed_ref[:, :384], own_out_ref[:, :384])
    total = total + dot_cols(mixed_ref[:, 384:], peer_out_ref[:, :384])
    middle_ref[...] = x_ref[...].astype(f32) + total + vec_ref[0:1]


def units_forward_kernel(middle_ref, own_ref, peer_ref, vec_ref, up_bias_ref, result_ref, active_ref, slope_ref):
    middle = middle_ref[...]
    normed, _ = norm_parts(middle)
    normed_b = (normed * vec_ref[4:5] + vec_ref[5:6]).astype(bf16)
    total = middle + vec_ref[1:2]
    for half, weight_ref in enumerate((own_ref, peer_ref)):
        for j in range(2):
            cols = slice(768 * (2 * half + j), 768 * (2 * half + j) + 768)
            pre_active = dot(normed_b, weight_ref[j]) + up_bias_ref[0:1, cols]
            below = 0.5 * (1.0 + lax.erf(pre_active * half_root))
            active_b = (pre_active * below).astype(bf16)
            active_ref[:, cols] = active_b
            slope_ref[:, cols] = below + pre_active * jnp.exp(-0.5 * pre_active * pre_active) * gauss_factor
            total = total + dot_cols(active_b, weight_ref[2 + j])
    result_ref[...] = total.astype(bf16)


def units_backward_kernel(
    grad_ref, middle_ref, active_ref, slope_ref, own_ref, peer_ref, vec_ref,
    grad_middle_ref, grad_own_ref, grad_peer_ref, vec_grad_ref, up_bias_grad_ref,
):
    grad_b = grad_ref[...]
    grad_rows = grad_b.astype(f32)
    normed, rescale = norm_parts(middle_ref[...])
    normed_b = (normed * vec_ref[4:5] + vec_ref[5:6]).astype(bf16)
    normed_t = normed_b.T
    grad_t = grad_b.T
    grad_normed = None
    for half, weight_ref, out_ref in ((1, peer_ref, grad_peer_ref), (0, own_ref, grad_own_ref)):
        for j in range(2):
            cols = slice(768 * (2 * half + j), 768 * (2 * half + j) + 768)
            out_ref[2 + j] = dot(grad_t, active_ref[:, cols]).astype(bf16)
            grad_upper = (dot(grad_b, weight_ref[2 + j]) * slope_ref[:, cols]).astype(bf16)
            up_bias_grad_ref[0:1, cols] = jnp.sum(grad_upper.astype(f32), 0, keepdims=True)
            out_ref[j] = dot(normed_t, grad_upper).astype(bf16)
            term = dot_cols(grad_upper, weight_ref[j])
            grad_normed = term if grad_normed is None else grad_normed + term
    grad_middle = grad_rows + norm_backward(grad_normed, normed, rescale, vec_ref[4:5])
    grad_middle_ref[...] = grad_middle
    vec_grad_ref[...] = jnp.zeros_like(vec_grad_ref)
    vec_grad_ref[0:1] = jnp.sum(grad_middle, 0, keepdims=True)
    vec_grad_ref[1:2] = jnp.sum(grad_rows, 0, keepdims=True)
    vec_grad_ref[4:5] = jnp.sum(grad_normed * normed, 0, keepdims=True)
    vec_grad_ref[5:6] = jnp.sum(grad_normed, 0, keepdims=True)


def attention_backward_kernel(
    grad_ref, x_ref, heads_ref, soft_ref, mixed_ref, own_ref, peer_ref, own_out_ref, peer_out_ref, vec_ref,
    grad_in_ref, grad_own_ref, grad_peer_ref, grad_own_out_ref, grad_peer_out_ref, vec_grad_ref,
    grad_mixed_ref, grad_heads_ref,
):
    grad_b = grad_ref[...].astype(bf16)
    grad_t = grad_b.T
    grad_peer_out_ref[...] = dot(grad_t, mixed_ref[:, 384:]).astype(bf16)
    grad_own_out_ref[...] = dot(grad_t, mixed_ref[:, :384]).astype(bf16)
    grad_mixed_ref[:, :384] = dot(grad_b, own_out_ref[:, :384]).astype(bf16)
    grad_mixed_ref[:, 384:] = dot(grad_b, peer_out_ref[:, :384]).astype(bf16)
    factor = HEAD ** (-0.5)
    for pair in range(6):
        found = ([], [], [])
        for head in (2 * pair, 2 * pair + 1):
            cols = slice(HEAD * head, HEAD * head + HEAD)
            soft = soft_ref[head]
            grad_head = grad_mixed_ref[:, cols]
            grad_soft = dot_cols(grad_head, heads_ref[2, :, cols])
            inner = jnp.sum(grad_soft * soft, -1, keepdims=True)
            grad_scores = (soft * (grad_soft - inner)).astype(bf16)
            found[0].append(dot(grad_scores, heads_ref[1, :, cols]) * factor)
            found[1].append(dot_rows(grad_scores, heads_ref[0, :, cols]) * factor)
            found[2].append(dot_rows(soft.astype(bf16), grad_head))
        for j in range(3):
            grad_heads_ref[j, :, 128 * pair : 128 * pair + 128] = jnp.concatenate(found[j], 1).astype(bf16)
    normed, rescale = norm_parts(x_ref[...].astype(f32))
    normed_b = (normed * vec_ref[2:3] + vec_ref[3:4]).astype(bf16)
    normed_t = normed_b.T
    grad_normed = None
    for half, weight_ref, out_ref in ((1, peer_ref, grad_peer_ref), (0, own_ref, grad_own_ref)):
        for j in range(3):
            rows = grad_heads_ref[j, :, 384 * half : 384 * half + 384]
            out_ref[j] = dot(normed_t, rows).astype(bf16)
            term = dot_cols(rows, weight_ref[j])
            grad_normed = term if grad_normed is None else grad_normed + term
    grad_in = grad_ref[...] + norm_backward(grad_normed, normed, rescale, vec_ref[2:3])
    grad_in_ref[...] = grad_in.astype(bf16)
    vec_grad_ref[...] = jnp.zeros_like(vec_grad_ref)
    vec_grad_ref[2:3] = jnp.sum(grad_normed * normed, 0, keepdims=True)
    vec_grad_ref[3:4] = jnp.sum(grad_normed, 0, keepdims=True)
    vec_grad_ref[6:7] = jnp.sum(grad_heads_ref[0].astype(f32), 0, keepdims=True)
    vec_grad_ref[7:8] = jnp.sum(grad_heads_ref[2].astype(f32), 0, keepdims=True)


def kernel_call(kernel, name, inputs, outputs, flops, scratch=(), scalar=False):
    whole = pl.BlockSpec(memory_space=pltpu.VMEM)
    specs = [whole] * len(inputs)
    if scalar:
        specs[0] = pl.BlockSpec(memory_space=pltpu.SMEM)
    shapes = [jax.ShapeDtypeStruct(shape, dtype) for shape, dtype in outputs]
    moved = sum(int(np.prod(a.shape)) * a.dtype.itemsize for a in list(inputs) + shapes)
    return pl.pallas_call(
        kernel,
        name=name,
        out_shape=shapes,
        in_specs=specs,
        out_specs=[whole] * len(shapes),
        scratch_shapes=list(scratch),
        cost_estimate=pl.CostEstimate(flops=flops, bytes_accessed=moved, transcendentals=0),
        compiler_params=pltpu.CompilerParams(vmem_limit_bytes=52 * 2**20),
    )(*inputs)


ROWS = (192, 768)
HEADS_SHAPE = (3, 192, 768)


def attention_forward(length, x, attn, vec):
    own, peer, own_out, peer_out = attn
    return kernel_call(
        attention_forward_kernel, "attention_forward",
        [length, x, own, peer, own_out, peer_out, vec],
        [(ROWS, f32), (HEADS_SHAPE, bf16), ((12, 192, 192), f32), (ROWS, bf16)],
        1_100_000_000, scalar=True,
    )


def units_forward(middle, units, vec, up_bias):
    own, peer = units
    return kernel_call(
        units_forward_kernel, "units_forward", [middle, own, peer, vec, up_bias],
        [(ROWS, bf16), ((192, 3072), bf16), ((192, 3072), f32)], 1_800_000_000,
    )


def units_backward(grad_b, middle, active, slope, units, vec):
    own, peer = units
    return kernel_call(
        units_backward_kernel, "units_backward", [grad_b, middle, active, slope, own, peer, vec],
        [(ROWS, f32), (own.shape, bf16), (peer.shape, bf16), ((8, 768), f32), ((1, 3072), f32)], 3_600_000_000,
    )


def attention_backward(grad_middle, x, heads, soft, mixed, attn, vec):
    own, peer, own_out, peer_out = attn
    return kernel_call(
        attention_backward_kernel, "attention_backward",
        [grad_middle, x, heads, soft, mixed, own, peer, own_out, peer_out, vec],
        [(ROWS, bf16), (own.shape, bf16), (peer.shape, bf16), ((768, 384), bf16), ((768, 384), bf16), ((8, 768), f32)],
        2_300_000_000,
        scratch=[pltpu.VMEM(ROWS, bf16), pltpu.VMEM(HEADS_SHAPE, bf16)],
    )


EXCHANGES = {"xu": ("x", 4, 1), "xv": ("x", 4, 3), "zu": ("z", 4, 1), "zv": ("z", 4, 3), "c": ("core", 2, 1)}
BLOCK_BITS = ("zv", "zu", "xv", "xu")
BIT_MASK = {"xu": 1, "xv": 3, "zu": 4, "zv": 12}
ORDERS = (
    ("xu", "xv", "zu", "zv"),
    ("xv", "xu", "zv", "zu"),
    ("zu", "zv", "xu", "xv"),
    ("zv", "zu", "xv", "xu"),
)
MASKS = np.zeros(16, np.int32)
for _index in range(16):
    for _place, _bit in enumerate(BLOCK_BITS):
        if (_index >> (3 - _place)) & 1:
            MASKS[_index] ^= BIT_MASK[_bit]
ATTN_COLS = (384, 384, 384, 512)


def exchange(value, bit):
    axis, size, flip = EXCHANGES[bit]
    return lax.ppermute(value, axis, [(i, i ^ flip) for i in range(size)])


def exchange_pipe(value):
    return lax.ppermute(value, "pipe", [(0, 1), (1, 0)])


def exchange_both(value):
    return lax.ppermute(value, ("pipe", "tensor"), [(i, i ^ 3) for i in range(4)])


def exchange_tensor(value):
    return lax.ppermute(value, "tensor", [(0, 1), (1, 0)])


def pin(*values):
    return lax.optimization_barrier(values)


def block_place(part, index):
    place = 0
    for step in range(4):
        if (index >> step) & 1:
            place += 8 >> BLOCK_BITS.index(ORDERS[part][step])
    return place


def assemble_kernel(counts, *refs):
    total = sum(counts)
    held, got, outs, sems = refs[:total], refs[total : 2 * total], refs[2 * total : -1], refs[-1]
    copies = []
    for part in range(total):
        if len(counts) == 1 or part < counts[0]:
            target = outs[0].at[part]
        else:
            target = outs[1]
        for index in range(16):
            source = (held if index < 8 else got)[part].at[index % 8]
            rows = target.at[pl.ds(48 * block_place(part, index), 48)]
            copies.append(pltpu.make_async_copy(source, rows, sems.at[len(copies)]))
            copies[-1].start()
    for copy in copies:
        copy.wait()


def assemble(held, got):
    cols = [part.shape[-1] for part in held]
    if cols[0] == cols[3]:
        counts, shapes = (4,), [(4, 768, cols[0])]
    else:
        counts, shapes = (3, 1), [(3, 768, cols[0]), (768, cols[3])]
    anywhere = pl.BlockSpec(memory_space=pl.ANY)
    return pl.pallas_call(
        functools.partial(assemble_kernel, counts),
        name="assemble",
        out_shape=[jax.ShapeDtypeStruct(shape, bf16) for shape in shapes],
        in_specs=[anywhere] * 8,
        out_specs=[anywhere] * len(shapes),
        scratch_shapes=[pltpu.SemaphoreType.DMA((64,))],
        cost_estimate=pl.CostEstimate(flops=0, bytes_accessed=2 * 768 * 2 * sum(cols), transcendentals=0),
    )(*held, *got)


def gather_start(own):
    pipe, core = lax.axis_index("pipe"), lax.axis_index("core")
    mine = jnp.where(core == 0, own[0], own[1])
    other = exchange(jnp.where(core == 0, own[1], own[0]), "c")
    rows = jnp.where(core == 0, jnp.concatenate([mine, other]), jnp.concatenate([other, mine]))
    other = exchange_pipe(rows)
    mine = jnp.stack([jnp.where(pipe == 0, rows, other), jnp.where(pipe == 0, other, rows)])
    theirs = exchange_both(mine)
    a, b = mine, theirs
    parts = [
        [a[..., :192], b[..., :192], a[..., 832:1600]],
        [a[..., 192:384], b[..., 192:384], b[..., 832:1600]],
        [a[..., 384:576], b[..., 384:576], a[..., 1600:]],
        [a[..., 576:768], b[..., 576:768], a[..., 768:832], b[..., 768:832], b[..., 1600:]],
    ]
    parts = [jnp.concatenate(part, -1)[:, None] for part in parts]
    for step in range(2):
        got = [exchange(part, ORDERS[i][step]) for i, part in enumerate(parts)]
        parts = [jnp.concatenate([x, y], 1) for x, y in zip(parts, got)]
    groups = []
    for layer in range(2):
        groups.append([part[layer, :, :, : ATTN_COLS[i]] for i, part in enumerate(parts)])
        groups.append([part[layer, :, :, ATTN_COLS[i] :] for i, part in enumerate(parts)])
    return groups


def gather_third(held):
    got = [exchange(part, ORDERS[i][2]) for i, part in enumerate(held)]
    return [jnp.concatenate([x, y], 0) for x, y in zip(held, got)]


def gather_fourth(held):
    return [exchange(part, ORDERS[i][3]) for i, part in enumerate(held)]


def gather_core(held, got):
    own = assemble(held, got)
    return own, [exchange(array, "c") for array in own]


def add(left_side, right_side):
    return (left_side.astype(f32) + right_side.astype(f32)).astype(bf16)


def halve(state, step):
    out = []
    for i, (names, x, y) in enumerate(state):
        bit = ORDERS[i][step]
        axis = names.index(bit) + x.ndim - 2 - len(names)
        keep, send = [add(lax.index_in_dim(x, side, axis, False), lax.index_in_dim(y, side, axis, False)) for side in (0, 1)]
        out.append((tuple(name for name in names if name != bit), keep, exchange(send, bit)))
    return out


def scatter_core(own, other):
    got = [exchange(array, "c") for array in other]
    state = []
    for x, y in zip(own, got):
        shape = (2, 2, 2, 2, 48, x.shape[-1])
        for_part = (lambda v: [v]) if x.ndim == 2 else list
        for u, v in zip(for_part(x), for_part(y)):
            state.append((BLOCK_BITS, u.reshape(shape), v.reshape(shape)))
    return state


def scatter_end(groups):
    pipe, core = lax.axis_index("pipe"), lax.axis_index("core")
    state = []
    for i in range(4):
        sides = []
        for side in (1, 2):
            layers = [jnp.concatenate([groups[2 * k][i][side], groups[2 * k + 1][i][side]], -1) for k in range(2)]
            sides.append(jnp.stack(layers))
        state.append((groups[0][i][0], *sides))
    state = halve(halve(state, 1), 0)
    p = [x.astype(f32) + y.astype(f32) for _, x, y in state]
    mine = [p[0][..., :192], p[1][..., :192], p[2][..., :192], p[3][..., :192], p[3][..., 384:448]]
    mine = jnp.concatenate(mine + [p[0][..., 384:], p[2][..., 384:]], -1)
    theirs = [p[0][..., 192:384], p[1][..., 192:384], p[2][..., 192:384], p[3][..., 192:384], p[3][..., 448:512]]
    theirs = jnp.concatenate(theirs + [p[1][..., 384:], p[3][..., 512:]], -1)
    total = mine + exchange_both(theirs.astype(bf16)).astype(f32)
    keep = jnp.where(pipe == 0, total[0], total[1])
    send = jnp.where(pipe == 0, total[1], total[0]).astype(bf16)
    rows = keep + exchange_pipe(send).astype(f32)
    keep = jnp.where(core == 0, rows[:24], rows[24:])
    send = jnp.where(core == 0, rows[24:], rows[:24]).astype(bf16)
    other = exchange(send, "c").astype(f32)
    return jnp.where(core == 0, keep, other), jnp.where(core == 0, other, keep)


def share_outputs(first_rows, second_rows):
    pipe, tensor = lax.axis_index("pipe"), lax.axis_index("tensor")
    keep = jnp.where(pipe == 0, first_rows, second_rows)
    send = jnp.where(pipe == 0, second_rows, first_rows)
    return keep, exchange_tensor(keep), exchange_pipe(send), exchange_both(send)


def order_outputs(rows):
    pipe, tensor = lax.axis_index("pipe"), lax.axis_index("tensor")
    a, b, c, d = rows
    a, b = jnp.where(tensor == 0, a, b), jnp.where(tensor == 0, b, a)
    c, d = jnp.where(tensor == 0, c, d), jnp.where(tensor == 0, d, c)
    a, c = jnp.where(pipe == 0, a, c), jnp.where(pipe == 0, c, a)
    b, d = jnp.where(pipe == 0, b, d), jnp.where(pipe == 0, d, b)
    return jnp.stack([a, b, c, d])[None]


def pack_share(w_query, w_key, w_value, w_out, w_up, w_down, b_query, b_value, b_up, vectors):
    cols = jnp.pad(jnp.stack(vectors, 1), ((0, 0), (0, 2)))
    out = []
    for half in range(2):
        third, sixth, whole = (slice(n * half, n * half + n) for n in (3, 12, 192))
        rows = jnp.concatenate([b_query[:, third], b_value[:, third], b_up[:, sixth]], 1)
        small = jnp.concatenate([cols, jnp.pad(rows, ((0, 22), (0, 38)))], 1)
        wide = slice(768 * half, 768 * half + 768)
        out.append(
            jnp.concatenate(
                [w_query[:, whole], w_key[:, whole], w_value[:, whole], w_out[:, whole], small, w_up[:, wide], w_down[:, wide]],
                1,
            )
        )
    return out


def unpack_share(halves):
    def cols(start, stop):
        return jnp.concatenate([half[:, start:stop] for half in halves], 1)

    grads = [cols(192 * i, 192 * i + 192) for i in range(4)] + [cols(832, 1600), cols(1600, 2368)]
    rows = [half[:2, 776:794] for half in halves]
    bias = [jnp.concatenate([row[:, lo:hi] for row in rows], 1) for lo, hi in ((0, 3), (3, 6), (6, 18))]
    return grads, bias, [halves[0][:, 768 + i] for i in range(6)]


def spread_small(own_out, peer_out, place_units):
    vectors = own_out[:, 384:390].astype(f32).T
    rows = jnp.concatenate([own_out[:, 384:], peer_out[:, 384:]], 1).reshape(32, 24, 4, 64)[:, :2, :, 8:26]
    rows = dot(place_units, rows.reshape(64, 72)).reshape(64, 4, 18).transpose(1, 2, 0)
    b_query, b_value = rows[:, :3].reshape(1, 768), rows[:, 3:6].reshape(1, 768)
    return jnp.concatenate([vectors, b_query, b_value]), rows[:, 6:].reshape(1, 3072)


def gather_small(vec_grad, up_bias_grad, place_units):
    rows = jnp.concatenate(
        [vec_grad[6].reshape(4, 3, HEAD), vec_grad[7].reshape(4, 3, HEAD), up_bias_grad.reshape(4, 12, HEAD)], 1
    )
    rows = rows.transpose(2, 0, 1).reshape(HEAD, 72).astype(bf16)
    rows = dot_rows(place_units, rows).astype(bf16).reshape(32, 2, 4, 18)
    rows = jnp.pad(rows, ((0, 0), (0, 22), (0, 0), (8, 38))).reshape(768, 256)
    cols = jnp.pad(vec_grad[:6].T.astype(bf16), ((0, 0), (0, 58)))
    small = rows + jnp.concatenate([cols] * 4, 1)
    return small[:, :128], small[:, 128:]


def local(clip_frames, out_cotangent, clip_lengths, *params):
    params = [param[0] for param in params]
    w_query, w_key, w_value, w_out, w_up, w_down, b_query, b_value, b_out, b_up, b_down = params[:11]
    micro = lax.axis_index("pipe") * 2 + lax.axis_index("tensor")
    chip = lax.axis_index("z") * 4 + lax.axis_index("x")

    blocks = (chip ^ jnp.asarray(MASKS))[:, None]
    rows_at = (blocks * 48 + jnp.arange(48)[None]).reshape(-1)
    place_rows = (jnp.arange(768)[:, None] == rows_at[None]).astype(bf16)
    units_at = (blocks * 4 + jnp.arange(4)[None]).reshape(-1)
    place_units = (jnp.arange(64)[:, None] == units_at[None]).astype(bf16)

    own = pack_share(
        w_query, w_key, w_value, w_out, w_up, w_down, b_query, b_value, b_up, [b_out, b_down] + params[11:]
    )
    groups = gather_start(own)

    frames = lax.dynamic_index_in_dim(clip_frames, micro, 0, keepdims=False)
    cotangent = lax.dynamic_index_in_dim(out_cotangent, micro, 0, keepdims=False)
    length = lax.dynamic_index_in_dim(clip_lengths, micro, 0, keepdims=False)
    x_first = dot(frames, place_rows).astype(bf16)
    grad_out = dot(cotangent, place_rows).astype(bf16)

    def placed_back(rows):
        return dot_cols(rows, place_rows).astype(bf16)

    def attn_of(own, peer):
        return own[0], peer[0], own[1], peer[1]

    held = [gather_third(group) for group in groups]
    got = [gather_fourth(held[0]), gather_fourth(held[1])]
    attn_first = attn_of(*gather_core(held[0], got[0]))
    vec_first, up_bias_first = spread_small(attn_first[2], attn_first[3], place_units)
    middle_first, heads_first, soft_first, mixed_first = attention_forward(length, x_first, attn_first, vec_first)
    units_first = [array[0] for array in gather_core(held[1], got[1])]
    got.append(gather_fourth(held[2]))
    middle_first, got[2] = pin(middle_first, got[2])
    x_second, active_first, slope_first = units_forward(middle_first, units_first, vec_first, up_bias_first)
    attn_second = attn_of(*gather_core(held[2], got[2]))
    got.append(gather_fourth(held[3]))
    x_second, got[3] = pin(x_second, got[3])
    vec_second, up_bias_second = spread_small(attn_second[2], attn_second[3], place_units)
    middle_second, heads_second, soft_second, mixed_second = attention_forward(length, x_second, attn_second, vec_second)
    units_second = [array[0] for array in gather_core(held[3], got[3])]
    out_second, active_second, slope_second = units_forward(middle_second, units_second, vec_second, up_bias_second)
    shared = share_outputs(placed_back(x_second), placed_back(out_second))

    grad_middle, grad_own, grad_peer, vec_grad_second, up_bias_grad = units_backward(
        grad_out, middle_second, active_second, slope_second, units_second, vec_second
    )
    units_state = [None, scatter_core([grad_own], [grad_peer])]
    second_grad, grad_own, grad_peer, grad_own_out, grad_peer_out, vec_grad = attention_backward(
        grad_middle, x_second, heads_second, soft_second, mixed_second, attn_second, vec_second
    )
    small_own, small_peer = gather_small(vec_grad_second + vec_grad, up_bias_grad, place_units)
    grad_own_out = jnp.concatenate([grad_own_out, small_own], 1)
    grad_peer_out = jnp.concatenate([grad_peer_out, small_peer], 1)
    second_grad, units_state[1], shared = pin(second_grad, [s[1:] for s in units_state[1]], shared)
    units_state[1] = [(BLOCK_BITS, *s) for s in units_state[1]]
    section_output = order_outputs(shared)
    attn_state = [None, scatter_core([grad_own, grad_own_out], [grad_peer, grad_peer_out])]

    units_state[1] = halve(units_state[1], 3)
    grad_middle, grad_own, grad_peer, vec_grad_first, up_bias_grad = units_backward(
        second_grad, middle_first, active_first, slope_first, units_first, vec_first
    )
    names = [[s[0] for s in units_state[1]], [s[0] for s in attn_state[1]]]
    grad_middle, values = pin(grad_middle, ([s[1:] for s in units_state[1]], [s[1:] for s in attn_state[1]]))
    units_state[1] = [(name, *s) for name, s in zip(names[0], values[0])]
    attn_state[1] = [(name, *s) for name, s in zip(names[1], values[1])]
    units_state[1] = halve(units_state[1], 2)
    attn_state[1] = halve(attn_state[1], 3)
    units_state[0] = scatter_core([grad_own], [grad_peer])
    first_grad, grad_own, grad_peer, grad_own_out, grad_peer_out, vec_grad = attention_backward(
        grad_middle, x_first, heads_first, soft_first, mixed_first, attn_first, vec_first
    )
    states = (units_state[1], attn_state[1], units_state[0])
    names = [[s[0] for s in state] for state in states]
    grad_own, grad_peer, values = pin(grad_own, grad_peer, [[s[1:] for s in state] for state in states])
    units_state[1], attn_state[1], units_state[0] = [
        [(name, *s) for name, s in zip(some, state)] for some, state in zip(names, values)
    ]
    small_own, small_peer = gather_small(vec_grad_first + vec_grad, up_bias_grad, place_units)
    grad_own_out = jnp.concatenate([grad_own_out, small_own], 1)
    grad_peer_out = jnp.concatenate([grad_peer_out, small_peer], 1)
    attn_state[0] = scatter_core([grad_own, grad_own_out], [grad_peer, grad_peer_out])
    units_state[0] = halve(halve(units_state[0], 3), 2)
    attn_state[1] = halve(attn_state[1], 2)
    attn_state[0] = halve(halve(attn_state[0], 3), 2)
    input_grad = order_outputs(share_outputs(placed_back(first_grad), placed_back(second_grad)))

    halves = scatter_end([attn_state[0], units_state[0], attn_state[1], units_state[1]])
    grads, bias, vectors = unpack_share(halves)
    grads = grads + [bias[0], bias[1], vectors[0], bias[2]] + vectors[1:]
    return (section_output, input_grad) + tuple(grad[None] for grad in grads)


def solution(mesh):
    fine = Mesh(mesh.devices.reshape(2, 4, 4, 2, 2), ("pipe", "z", "x", "core", "tensor"))
    shard = ("z", "x", "core")
    rows = P(None, shard, None)
    matrix = P("pipe", shard, "tensor")
    vector = P("pipe", shard)
    params = (matrix,) * 8 + (vector, matrix) + (vector,) * 5
    return jax.shard_map(
        local,
        mesh=fine,
        in_specs=(rows, rows, P(None, shard)) + params,
        out_specs=(P("pipe", None, shard, None),) * 2 + params,
        check_vma=False,
    )
```

time: 606 us -> 935 us (1.54)
  Pallas kernels: 0 us -> 528 us
  matrix products: 98.5 us -> 6.94 us
  local copies, waits for them, and re-layouts: 124 us -> 54.3 us
  waiting for transfers between devices: 219 us -> 175 us
  starting transfers between devices: 89.1 us -> 101 us
    pallas_call x0 -> x12, Pallas kernels: none -> 528 us  [the longest x4 447 us: assemble(): pl.pallas_call(functools.partial(assemble_kernel, counts), name='assemble...]
    dot_general x43 -> x10, matrix products: 93.7 us -> 6.94 us  [the longest x4 4.14 us: dot_cols(): lax.dot_general(left_side, right_side, (((1,), (1,)), ((), ())), preferre...]
    slice x41 -> x58, local copies, waits for them, and re-layouts: 59.7 us -> 12.2 us  [the longest x2 1.88 us: spread_small(): jnp.concatenate([own_out[:, 384:], peer_out[:, 384:]], 1)]
    ppermute x64 -> x94, waiting for transfers between devices: 195 us -> 149 us  [exchange(): return lax.ppermute(value, axis, [(i, i ^ flip) for i in range(size)])]
    concatenate x4 -> x8, local copies, waits for them, and re-layouts: 15.4 us -> 1.4 us  [the longest x4 0.42 us: gather_start(): parts = [jnp.concatenate(part, -1)[:, None] for part in parts]]
    ppermute x64 -> x94, starting transfers between devices: 73.8 us -> 85.8 us  [exchange(): return lax.ppermute(value, axis, [(i, i ^ flip) for i in range(size)])]
    another operation x27 -> x14, local copies, waits for them, and re-layouts: 7.71 us -> 19.3 us  [the longest x4 9.86 us: scatter_core(): for_part(x)]
    squeeze x30 -> x0, local copies, waits for them, and re-layouts: 9.37 us -> none  [the longest x6 8.32 us: scatter_plane_large(): got = [exchange(part[1], 'c') for part in out]]
  transfers between devices with their start and end apart: 74 -> 104, of which waited for: 32 -> 46; matrix products, arithmetic and copies ran while one was open for 34% -> 10% of each run, Pallas kernels for 0% -> 24%
where the time goes in v2:
time: 935 us; the launch traced here: 924 us
  Pallas kernels  528 us (56%)
  waiting for transfers between devices  175 us (19%)
  starting transfers between devices  101 us (11%)
  other arithmetic  56.6 us (6%)
  local copies, waits for them, and re-layouts  54.3 us (6%)
    pallas_call x4, Pallas kernels, assemble(): pl.pallas_call(functools.partial(assemble_kernel, counts), name='assemble...  447 us
    ppermute x94, waiting for transfers between devices, exchange(): return lax.ppermute(value, axis, [(i, i ^ flip) for i in range(size)])  149 us
    ppermute x94, starting transfers between devices, exchange(): return lax.ppermute(value, axis, [(i, i ^ flip) for i in range(size)])  85.8 us
    pallas_call x8, Pallas kernels, kernel_call(): pl.pallas_call(kernel, name=name, out_shape=shapes, in_specs=specs, out_s...  80 us
    convert_element_type x44, other arithmetic, add(): return (left_side.astype(f32) + right_side.astype(f32)).astype(bf16)  21.8 us
  transfers between devices with their start and end apart: 104, of which 46 were waited for; matrix products, arithmetic and copies ran while one was open for 10% of the time, Pallas kernels for 24%

profile of v2, /device:TPU:0, one launch (start us, length us, event | category | flops | bytes accessed | tf_op | source)
XLA Modules:
  0.0 923.9 jit_solution(5129298579695789838)
XLA Ops:
  10.2 6.1 collective-permute-done.1
  19.8 9.9 %collective-permute-done.2 = bf16[2,48,2368]{2,1,0:T(8,128)(2,1)S(1)} collective-permute-done((bf16[2,48,2368]{2,1,0:T(8,128)(2,1)S(1)}, bf16[2,48,2368]{2,1,0:T(8,128)(2,1)S(1)}, u32[]{:S(2)}, u32[]{:S(2)}) %collective-permute-start.2) | collective-permute-done | bytes 454688 | tf_op jit(solution)/shard_map/ppermute | solution.py:258
  70.8 6.7 collective-permute-done.35.refs_6_
  80.5 144.6 %assemble.5.own_ref = bf16[4,768,768]{2,1,0:T(8,128)(2,1)} custom-call(bf16[8,48,768]{2,1,0:T(8,128)(2,1)} %copy-done.14, bf16[8,48,768]{2,1,0:T(8,128)(2,1)} %copy-done.13, bf16[8,48,768]{2,1,0:T(8,128)(2,1)} %copy-done.12, bf16[8,48,768]{2,1,0:T(8,128)(2,1)} %copy-done.15, bf16[8,48,768]{2,1,0:T(8,128)(2,1)} %copy-done.55, bf16[8,48,768]{2,1,0:T(8,128)(2,1)} %copy-done.54, ...), custom_call_target="tpu_custom_call" | custom-call | bytes 9437184 | tf_op jit(solution)/shard_map/assemble/pallas_call | solution.py:302
  253.3 79.1 %assemble.4 = (bf16[3,768,384]{2,1,0:T(8,128)(2,1)}, bf16[768,512]{1,0:T(8,128)(2,1)}) custom-call(bf16[8,48,384]{2,1,0:T(8,128)(2,1)} %copy-done.44, bf16[8,48,384]{2,1,0:T(8,128)(2,1)} %copy-done.43, bf16[8,48,384]{2,1,0:T(8,128)(2,1)} %copy-done.42, bf16[8,48,512]{2,1,0:T(8,128)(2,1)} %copy-done.40, bf16[8,48,384]{2,1,0:T(8,128)(2,1)} %collective-permute-done.15.refs_4_, ...), custom_call_target="tpu_custom_call" | custom-call | bytes 5111808 | tf_op jit(solution)/shard_map/assemble/pallas_call | solution.py:302
  374.4 7.6 attention_forward.2
  382.0 8.1 units_forward.2
  390.1 144.6 %assemble.7.own_ref = bf16[4,768,768]{2,1,0:T(8,128)(2,1)} custom-call(bf16[8,48,768]{2,1,0:T(8,128)(2,1)} %pad_maximum_fusion.9.refs_0_, bf16[8,48,768]{2,1,0:T(8,128)(2,1)} %pad_maximum_fusion.10.refs_1_, bf16[8,48,768]{2,1,0:T(8,128)(2,1)} %copy-done.11, bf16[8,48,768]{2,1,0:T(8,128)(2,1)} %pad_maximum_fusion.12.refs_3_, ...), custom_call_target="tpu_custom_call" | custom-call | bytes 9437184 | tf_op jit(solution)/shard_map/assemble/pallas_call | solution.py:302
  534.9 79.1 %assemble.6 = (bf16[3,768,384]{2,1,0:T(8,128)(2,1)}, bf16[768,512]{1,0:T(8,128)(2,1)}) custom-call(bf16[8,48,384]{2,1,0:T(8,128)(2,1)} %pad_maximum_fusion.40.refs_0_, bf16[8,48,384]{2,1,0:T(8,128)(2,1)} %pad_maximum_fusion.41.refs_1_, bf16[8,48,384]{2,1,0:T(8,128)(2,1)} %copy-done.41, bf16[8,48,512]{2,1,0:T(8,128)(2,1)} %copy-done.39, ...), custom_call_target="tpu_custom_call" | custom-call | bytes 5111808 | tf_op jit(solution)/shard_map/assemble/pallas_call | solution.py:302
  623.2 7.7 attention_forward.3
  630.9 8.1 units_forward.3
  639.0 11.7 %units_backward.2 = (f32[192,768]{1,0:T(8,128)S(1)}, bf16[4,768,768]{2,1,0:T(8,128)(2,1)}, bf16[4,768,768]{2,1,0:T(8,128)(2,1)}, f32[8,768]{1,0:T(8,128)S(1)}, f32[1,3072]{1,0:T(1,128)S(1)}) custom-call(bf16[192,768]{1,0:T(8,128)(2,1)S(1)} %fusion.6.grad_ref, f32[192,768]{1,0:T(8,128)S(1)} %get-tuple-element.135.middle_ref, ...), custom_call_target="tpu_custom_call" | custom-call | flops 3600000000 | bytes 23949312 | tf_op jit(solution)/shard_map/units_backward/pallas_call | solution.py:178
  656.9 12.5 %attention_backward.2 = (bf16[192,768]{1,0:T(8,128)(2,1)S(1)}, bf16[3,768,384]{2,1,0:T(8,128)(2,1)}, bf16[3,768,384]{2,1,0:T(8,128)(2,1)}, bf16[768,384]{1,0:T(8...) custom-call(f32[192,768]{1,0:T(8,128)} %copy-done.5, bf16[192,768]{1,0:T(8,128)(2,1)S(1)} %get-tuple-element.128.x_ref, ...), custom_call_target="tpu_custom_call" | custom-call | flops 2300000000 | bytes 14008320 | tf_op jit(solution)/shard_map/attention_backward/pallas_call | solution.py:178
  703.3 11.7 %units_backward.3 = (f32[192,768]{1,0:T(8,128)S(1)}, bf16[4,768,768]{2,1,0:T(8,128)(2,1)}, bf16[4,768,768]{2,1,0:T(8,128)(2,1)}, f32[8,768]{1,0:T(8,128)S(1)}, f32[1,3072]{1,0:T(1,128)S(1)}) custom-call(bf16[192,768]{1,0:T(8,128)(2,1)S(1)} %get-tuple-element.154.grad_ref, f32[192,768]{1,0:T(8,128)S(1)} %get-tuple-element.126.middle_ref, ...), custom_call_target="tpu_custom_call" | custom-call | flops 3600000000 | bytes 23949312 | tf_op jit(solution)/shard_map/units_backward/pallas_call | solution.py:178
  730.3 12.5 %attention_backward.3 = (bf16[192,768]{1,0:T(8,128)(2,1)S(1)}, bf16[3,768,384]{2,1,0:T(8,128)(2,1)}, bf16[3,768,384]{2,1,0:T(8,128)(2,1)}, bf16[768,384]{1,0:T(8...) custom-call(f32[192,768]{1,0:T(8,128)} %copy-done.4, bf16[192,768]{1,0:T(8,128)(2,1)S(1)} %fusion.7.x_ref, ...), custom_call_target="tpu_custom_call" | custom-call | flops 2300000000 | bytes 14008320 | tf_op jit(solution)/shard_map/attention_backward/pallas_call | solution.py:178
  758.7 9.4 %collective-permute-done.94 = bf16[2,2,2,48,512]{4,3,0,1,2:T(8,128)(2,1)S(1)} collective-permute-done((bf16[2,2,2,48,512]{4,3,0,1,2:T(8,128)(2,1)S(1)}, bf16[2,2,2,48,512]{4,3,0,1,2:T(8,128)(2,1)S(1)}, u32[]{:S(2)}, u32[]{:S(2)}) %collective-permute-start.94) | collective-permute-done | bytes 393248 | tf_op jit(solution)/shard_map/ppermute | solution.py:250
  779.6 5.5 collective-permute-done.64
  796.2 8.0 collective-permute-done.90
  810.6 6.0 collective-permute-done.76
  820.8 13.2 %collective-permute-done.97 = bf16[2,2,48,768]{3,2,0,1:T(8,128)(2,1)S(1)} collective-permute-done((bf16[2,2,48,768]{3,2,0,1:T(8,128)(2,1)S(1)}, bf16[2,2,48,768]{3,2,0,1:T(8,128)(2,1)S(1)}, u32[]{:S(2)}, u32[]{:S(2)}) %collective-permute-start.97) | collective-permute-done | bytes 294944 | tf_op jit(solution)/shard_map/ppermute | solution.py:250
  836.3 9.8 %collective-permute-done.99 = bf16[2,2,48,1280]{3,2,0,1:T(8,128)(2,1)S(1)} collective-permute-done((bf16[2,2,48,1280]{3,2,0,1:T(8,128)(2,1)S(1)}, bf16[2,2,48,1280]{3,2,0,1:T(8,128)(2,1)S(1)}, u32[]{:S(2)}, u32[]{:S(2)}) %collective-permute-start.99) | collective-permute-done | bytes 491552 | tf_op jit(solution)/shard_map/ppermute | solution.py:250
  847.3 6.3 collective-permute-done.100
  855.5 6.7 collective-permute-done.86
  863.9 9.4 %collective-permute-done.72 = bf16[2,2,2,48,384]{4,3,2,1,0:T(8,128)(2,1)S(1)} collective-permute-done((bf16[2,2,2,48,384]{4,3,2,1,0:T(8,128)(2,1)S(1)}, bf16[2,2,2,48,384]{4,3,2,1,0:T(8,128)(2,1)S(1)}, u32[]{:S(2)}, u32[]{:S(2)}) %collective-permute-start.72) | collective-permute-done | bytes 294944 | tf_op jit(solution)/shard_map/ppermute | solution.py:250
  (585 shorter events, 296.3 us)
Async XLA Ops:
  225.2 156.8 %collective-permute-start.37 = (bf16[4,768,768]{2,1,0:T(8,128)(2,1)}, bf16[4,768,768]{2,1,0:T(8,128)(2,1)}, u32[]{:S(2)}, u32[]{:S(2)}) collective-permute-start(bf16[4,768,768]{2,1,0:T(8,128)(2,1)} %assemble.5.own_ref), channel_id=1, source_target_pairs={{0,2},{2,0},{1,3},{3,1},{4,6},{6,4},{5,7},{7,5},{8,10},{10,8},{9,1... | collective-permute-start | bytes 14155784 | tf_op jit(solution)/shard_map/ppermute | solution.py:250
  247.8 85.4 %collective-permute-start.25 = (bf16[4,48,384]{2,1,0:T(8,128)(2,1)}, bf16[4,48,384]{2,1,0:T(8,128)(2,1)S(1)}, u32[]{:S(2)}, u32[]{:S(2)}) collective-permute-start(bf16[4,48,384]{2,1,0:T(8,128)(2,1)} %get-tuple-element.335), channel_id=1, source_target_pairs={{0,4},{4,0},{8,12},{12,8},{1,5},{5,1},{9,13},{13,9},{2,6},{6,2},{1... | collective-permute-start | bytes 442376 | tf_op jit(solution)/shard_map/ppermute | solution.py:250
  248.3 86.3 %collective-permute-start.23 = (bf16[4,48,384]{2,1,0:T(8,128)(2,1)S(1)}, bf16[4,48,384]{2,1,0:T(8,128)(2,1)S(1)}, u32[]{:S(2)}, u32[]{:S(2)}) collective-permute-start(bf16[4,48,384]{2,1,0:T(8,128)(2,1)S(1)} %copy-done.56), channel_id=1, source_target_pairs={{0,48},{16,32},{32,16},{48,0},{1,49},{17,33},{33,17},{49,1},{2,50}... | collective-permute-start | bytes 442376 | tf_op jit(solution)/shard_map/ppermute | solution.py:250
  249.2 86.7 %collective-permute-start.21 = (bf16[4,48,384]{2,1,0:T(8,128)(2,1)}, bf16[4,48,384]{2,1,0:T(8,128)(2,1)S(1)}, u32[]{:S(2)}, u32[]{:S(2)}) collective-permute-start(bf16[4,48,384]{2,1,0:T(8,128)(2,1)} %get-tuple-element.339), channel_id=1, source_target_pairs={{0,16},{16,0},{32,48},{48,32},{1,17},{17,1},{33,49},{49,33},{2,18}... | collective-permute-start | bytes 442376 | tf_op jit(solution)/shard_map/ppermute | solution.py:250
  332.4 41.2 %collective-permute-start.19 = (bf16[3,768,384]{2,1,0:T(8,128)(2,1)}, bf16[3,768,384]{2,1,0:T(8,128)(2,1)}, u32[]{:S(2)}, u32[]{:S(2)}) collective-permute-start(bf16[3,768,384]{2,1,0:T(8,128)(2,1)} %get-tuple-element.123.own_ref), channel_id=1, source_target_pairs={{0,2},{2,0},{1,3},{3,1},{4,6},{6,4},{5,7},{7,5},{8,10},{10,8},{9,1... | collective-permute-start | bytes 5308424 | tf_op jit(solution)/shard_map/ppermute | solution.py:250
  534.8 96.1 %collective-permute-start.48 = (bf16[4,768,768]{2,1,0:T(8,128)(2,1)}, bf16[4,768,768]{2,1,0:T(8,128)(2,1)}, u32[]{:S(2)}, u32[]{:S(2)}) collective-permute-start(bf16[4,768,768]{2,1,0:T(8,128)(2,1)} %assemble.7.own_ref), channel_id=1, source_target_pairs={{0,2},{2,0},{1,3},{3,1},{4,6},{6,4},{5,7},{7,5},{8,10},{10,8},{9,1... | collective-permute-start | bytes 14155784 | tf_op jit(solution)/shard_map/ppermute | solution.py:250
  651.6 35.4 %collective-permute-start.49 = (bf16[4,768,768]{2,1,0:T(8,128)(2,1)}, bf16[4,768,768]{2,1,0:T(8,128)(2,1)}, u32[]{:S(2)}, u32[]{:S(2)}) collective-permute-start(bf16[4,768,768]{2,1,0:T(8,128)(2,1)} %get-tuple-element.148), channel_id=1, source_target_pairs={{0,2},{2,0},{1,3},{3,1},{4,6},{6,4},{5,7},{7,5},{8,10},{10,8},{9,1... | collective-permute-start | bytes 14155784 | tf_op jit(solution)/shard_map/ppermute | solution.py:250
  654.0 39.1 %collective-permute-start.51 = (bf16[192,768]{1,0:T(8,128)(2,1)}, bf16[192,768]{1,0:T(8,128)(2,1)}, u32[]{:S(2)}, u32[]{:S(2)}) collective-permute-start(bf16[192,768]{1,0:T(8,128)(2,1)} %get-tuple-element.369), channel_id=1, source_target_pairs={{0,64},{64,0},{1,65},{65,1},{2,66},{66,2},{3,67},{67,3},{4,68},{68... | collective-permute-start | bytes 884744 | tf_op jit(solution)/shard_map/ppermute | solution.py:254
  654.2 38.9 %collective-permute-start.52 = (bf16[192,768]{1,0:T(8,128)(2,1)}, bf16[192,768]{1,0:T(8,128)(2,1)}, u32[]{:S(2)}, u32[]{:S(2)}) collective-permute-start(bf16[192,768]{1,0:T(8,128)(2,1)} %get-tuple-element.369), channel_id=1, source_target_pairs={{0,65},{1,64},{64,1},{65,0},{2,67},{3,66},{66,3},{67,2},{4,69},{5,... | collective-permute-start | bytes 884744 | tf_op jit(solution)/shard_map/ppermute | solution.py:258
  675.2 46.9 %collective-permute-start.58 = (bf16[768,512]{1,0:T(8,128)(2,1)}, bf16[768,512]{1,0:T(8,128)(2,1)}, u32[]{:S(2)}, u32[]{:S(2)}) collective-permute-start(bf16[768,512]{1,0:T(8,128)(2,1)} %pad_maximum_fusion.2), channel_id=1, source_target_pairs={{0,2},{2,0},{1,3},{3,1},{4,6},{6,4},{5,7},{7,5},{8,10},{10,8},{9,1... | collective-permute-start | bytes 2359304 | tf_op jit(solution)/shard_map/ppermute | solution.py:250
  694.5 27.6 %collective-permute-start.56 = (bf16[2,2,2,48,768]{4,3,0,1,2:T(8,128)(2,1)}, bf16[2,2,2,48,768]{4,3,0,1,2:T(8,128)(2,1)}, u32[]{:S(2)}, u32[]{:S(2)}) collective-permute-start(bf16[2,2,2,48,768]{4,3,0,1,2:T(8,128)(2,1)} %get-tuple-element.267), channel_id=1, source_target_pairs={{0,4},{4,0},{8,12},{12,8},{1,5},{5,1},{9,13},{13,9},{2,6},{6,2},{1... | collective-permute-start | bytes 1769480 | tf_op jit(solution)/shard_map/ppermute | solution.py:250
  697.8 24.3 %collective-permute-start.55 = (bf16[2,2,2,48,768]{4,3,1,0,2:T(8,128)(2,1)}, bf16[2,2,2,48,768]{4,3,1,0,2:T(8,128)(2,1)}, u32[]{:S(2)}, u32[]{:S(2)}) collective-permute-start(bf16[2,2,2,48,768]{4,3,1,0,2:T(8,128)(2,1)} %get-tuple-element.269), channel_id=1, source_target_pairs={{0,12},{4,8},{8,4},{12,0},{1,13},{5,9},{9,5},{13,1},{2,14},{6,10},... | collective-permute-start | bytes 1769480 | tf_op jit(solution)/shard_map/ppermute | solution.py:250
  722.1 50.5 %collective-permute-start.70 = (bf16[4,768,768]{2,1,0:T(8,128)(2,1)}, bf16[4,768,768]{2,1,0:T(8,128)(2,1)}, u32[]{:S(2)}, u32[]{:S(2)}) collective-permute-start(bf16[4,768,768]{2,1,0:T(8,128)(2,1)} %get-tuple-element.197), channel_id=1, source_target_pairs={{0,2},{2,0},{1,3},{3,1},{4,6},{6,4},{5,7},{7,5},{8,10},{10,8},{9,1... | collective-permute-start | bytes 14155784 | tf_op jit(solution)/shard_map/ppermute | solution.py:250
  723.2 45.3 %collective-permute-start.68 = (bf16[2,2,2,48,384]{4,3,1,0,2:T(8,128)(2,1)}, bf16[2,2,2,48,384]{4,3,1,0,2:T(8,128)(2,1)}, u32[]{:S(2)}, u32[]{:S(2)}) collective-permute-start(bf16[2,2,2,48,384]{4,3,1,0,2:T(8,128)(2,1)} %get-tuple-element.303), channel_id=1, source_target_pairs={{0,12},{4,8},{8,4},{12,0},{1,13},{5,9},{9,5},{13,1},{2,14},{6,10},... | collective-permute-start | bytes 884744 | tf_op jit(solution)/shard_map/ppermute | solution.py:250
  726.0 43.6 %collective-permute-start.67 = (bf16[2,2,2,48,384]{4,3,1,2,0:T(8,128)(2,1)}, bf16[2,2,2,48,384]{4,3,1,2,0:T(8,128)(2,1)}, u32[]{:S(2)}, u32[]{:S(2)}) collective-permute-start(bf16[2,2,2,48,384]{4,3,1,2,0:T(8,128)(2,1)} %get-tuple-element.305), channel_id=1, source_target_pairs={{0,16},{16,0},{32,48},{48,32},{1,17},{17,1},{33,49},{49,33},{2,18}... | collective-permute-start | bytes 884744 | tf_op jit(solution)/shard_map/ppermute | solution.py:250
  728.1 42.7 %collective-permute-start.66 = (bf16[2,2,2,48,384]{4,3,2,1,0:T(8,128)(2,1)}, bf16[2,2,2,48,384]{4,3,2,1,0:T(8,128)(2,1)}, u32[]{:S(2)}, u32[]{:S(2)}) collective-permute-start(bf16[2,2,2,48,384]{4,3,2,1,0:T(8,128)(2,1)} %get-tuple-element.307), channel_id=1, source_target_pairs={{0,48},{16,32},{32,16},{48,0},{1,49},{17,33},{33,17},{49,1},{2,50}... | collective-permute-start | bytes 884744 | tf_op jit(solution)/shard_map/ppermute | solution.py:250
  778.3 42.0 %collective-permute-start.96 = (bf16[2,2,48,512]{3,2,0,1:T(8,128)(2,1)S(1)}, bf16[2,2,48,512]{3,2,0,1:T(8,128)(2,1)S(1)}, u32[]{:S(2)}, u32[]{:S(2)}) collective-permute-start(bf16[2,2,48,512]{3,2,0,1:T(8,128)(2,1)S(1)} %get-tuple-element.342), channel_id=1, source_target_pairs={{0,12},{4,8},{8,4},{12,0},{1,13},{5,9},{9,5},{13,1},{2,14},{6,10},... | collective-permute-start | bytes 589832 | tf_op jit(solution)/shard_map/ppermute | solution.py:250
  786.9 29.9 %collective-permute-start.95 = (bf16[2,2,2,48,768]{4,3,0,1,2:T(8,128)(2,1)S(1)}, bf16[2,2,2,48,768]{4,3,0,1,2:T(8,128)(2,1)S(1)}, u32[]{:S(2)}, u32[]{:S(2)}) collective-permute-start(bf16[2,2,2,48,768]{4,3,0,1,2:T(8,128)(2,1)S(1)} %get-tuple-element.262), channel_id=1, source_target_pairs={{0,4},{4,0},{8,12},{12,8},{1,5},{5,1},{9,13},{13,9},{2,6},{6,2},{1... | collective-permute-start | bytes 1769480 | tf_op jit(solution)/shard_map/ppermute | solution.py:250
  787.6 29.5 %collective-permute-start.98 = (bf16[2,2,48,512]{3,2,0,1:T(8,128)(2,1)S(1)}, bf16[2,2,48,512]{3,2,0,1:T(8,128)(2,1)S(1)}, u32[]{:S(2)}, u32[]{:S(2)}) collective-permute-start(bf16[2,2,48,512]{3,2,0,1:T(8,128)(2,1)S(1)} %get-tuple-element.344), channel_id=1, source_target_pairs={{0,12},{4,8},{8,4},{12,0},{1,13},{5,9},{9,5},{13,1},{2,14},{6,10},... | collective-permute-start | bytes 589832 | tf_op jit(solution)/shard_map/ppermute | solution.py:250
  788.8 65.2 %collective-permute-start.71 = (bf16[3,768,384]{2,1,0:T(8,128)(2,1)S(1)}, bf16[3,768,384]{2,1,0:T(8,128)(2,1)S(1)}, u32[]{:S(2)}, u32[]{:S(2)}) collective-permute-start(bf16[3,768,384]{2,1,0:T(8,128)(2,1)S(1)} %copy-done.60), channel_id=1, source_target_pairs={{0,2},{2,0},{1,3},{3,1},{4,6},{6,4},{5,7},{7,5},{8,10},{10,8},{9,1... | collective-permute-start | bytes 5308424 | tf_op jit(solution)/shard_map/ppermute | solution.py:250
  820.3 26.7 %collective-permute-start.73 = (bf16[2,2,2,48,768]{4,3,2,1,0:T(8,128)(2,1)S(1)}, bf16[2,2,2,48,768]{4,3,2,1,0:T(8,128)(2,1)S(1)}, u32[]{:S(2)}, u32[]{:S(2)}) collective-permute-start(bf16[2,2,2,48,768]{4,3,2,1,0:T(8,128)(2,1)S(1)} %get-tuple-element.266), channel_id=1, source_target_pairs={{0,48},{16,32},{32,16},{48,0},{1,49},{17,33},{33,17},{49,1},{2,50}... | collective-permute-start | bytes 1769480 | tf_op jit(solution)/shard_map/ppermute | solution.py:250
  834.9 39.3 %collective-permute-start.89 = (bf16[2,2,48,768]{3,2,1,0:T(8,128)(2,1)S(1)}, bf16[2,2,48,768]{3,2,1,0:T(8,128)(2,1)S(1)}, u32[]{:S(2)}, u32[]{:S(2)}) collective-permute-start(bf16[2,2,48,768]{3,2,1,0:T(8,128)(2,1)S(1)} %get-tuple-element.298), channel_id=1, source_target_pairs={{0,4},{4,0},{8,12},{12,8},{1,5},{5,1},{9,13},{13,9},{2,6},{6,2},{1... | collective-permute-start | bytes 884744 | tf_op jit(solution)/shard_map/ppermute | solution.py:250
  835.1 42.1 %collective-permute-start.82 = (bf16[2,2,48,768]{3,2,0,1:T(8,128)(2,1)S(1)}, bf16[2,2,48,768]{3,2,0,1:T(8,128)(2,1)S(1)}, u32[]{:S(2)}, u32[]{:S(2)}) collective-permute-start(bf16[2,2,48,768]{3,2,0,1:T(8,128)(2,1)S(1)} %get-tuple-element.300), channel_id=1, source_target_pairs={{0,48},{16,32},{32,16},{48,0},{1,49},{17,33},{33,17},{49,1},{2,50}... | collective-permute-start | bytes 884744 | tf_op jit(solution)/shard_map/ppermute | solution.py:250
  847.2 32.9 %collective-permute-start.75 = (bf16[2,2,48,768]{3,2,1,0:T(8,128)(2,1)S(1)}, bf16[2,2,48,768]{3,2,1,0:T(8,128)(2,1)S(1)}, u32[]{:S(2)}, u32[]{:S(2)}) collective-permute-start(bf16[2,2,48,768]{3,2,1,0:T(8,128)(2,1)S(1)} %get-tuple-element.302), channel_id=1, source_target_pairs={{0,16},{16,0},{32,48},{48,32},{1,17},{17,1},{33,49},{49,33},{2,18}... | collective-permute-start | bytes 884744 | tf_op jit(solution)/shard_map/ppermute | solution.py:250
  (143 other events, 1940.6 us)
